TPU v7x, 32 devices: a whole 2x2x4 slice. The times are simulated.
32 devices in a mesh: rcv: 16 (over z, x, core), src: 2 (over y).
Axes of the slice: x: 2, y: 2, z: 4, core: 2. Of those that a mesh axis runs over, the one named last changes fastest.
Arguments:
- records: float32 [1024, 4096], P(('rcv', 'src')), may hold values from -6 to 6
- window_start: int32 [32], P(('rcv', 'src')), may hold values from 0 to 16
- channel_segment: int32 [1024], replicated, may hold values from 0 to 63, as said below
- segment_row: int32 [64], replicated, may hold values from 0 to 63, as said below
Outputs:
- stacks: float32 [64, 16, 256], P('rcv', 'src')
Inputs may be any that keep to these rules, and one draw needn't show every extreme that they name: `window_start`: window positions index the group's 64 channels with the tile's own 32 channels left out. A permutation: segment s is stacked into row segment_row[s], held by rcv index segment_row[s] // 4. `channel_segment`: the 32 channels of each tile (aligned blocks) lie in segments of exactly 16 rcv indices, exactly 2 channels for each; one rcv index receives 2 channels from every tile.
All inputs are finite; a program needn't handle non-finite values.
Results may differ from a plain program's by a relative error of at most 0.0058.
Values may be sent and summed in bfloat16 or wider, within the bound.
A program may use at most 64 MiB of HBM per device.

v0:
```python
import math

import jax
import jax.numpy as jnp
from jax import lax
from jax.sharding import PartitionSpec as P

NFFT = 1024
LAGS = 256
CAP = 2
SEG_PER = 4


def dft_table(length):
    sample_index = jnp.arange(length, dtype=jnp.int32)
    frequency = jnp.arange(length // 2, dtype=jnp.int32)
    angles = (sample_index[:, None] * frequency[None, :] % length).astype(jnp.float32) * (
        2.0 * math.pi / length
    )
    return jnp.concatenate([jnp.cos(angles), -jnp.sin(angles)], axis=1)


def lag_table(length, lag_count):
    frequency = jnp.arange(length // 2, dtype=jnp.int32)
    shifts = jnp.arange(lag_count, dtype=jnp.int32) - lag_count // 2
    angles = (frequency[:, None] * shifts[None, :] % length).astype(jnp.float32) * (
        2.0 * math.pi / length
    )
    return jnp.concatenate([jnp.cos(angles), -jnp.sin(angles)], axis=0).astype(jnp.bfloat16)


def whiten(spectrum):
    half_size = spectrum.shape[-1] // 2
    powers = spectrum[..., :half_size] ** 2 + spectrum[..., half_size:] ** 2
    mean_power = jnp.mean(powers, axis=-1, keepdims=True)
    magnitude = jnp.sqrt(powers + 0.1 * mean_power + 1e-06)
    return spectrum / jnp.concatenate([magnitude, magnitude], axis=-1)


def correlate(own_tile, sources, lag_rows, block_count):
    half_size = own_tile.shape[-1] // 2
    left_re, left_im = (own_tile[..., :half_size], own_tile[..., half_size:])
    right_re, right_im = (sources[..., :half_size], sources[..., half_size:])

    def product(left_part, right_part):
        return jnp.einsum("ibf,jbf->ijf", left_part, right_part, preferred_element_type=jnp.float32)

    real_part = product(left_re, right_re) + product(left_im, right_im)
    imag_part = product(left_re, right_im) - product(left_im, right_re)
    cross_spec = jnp.concatenate([real_part, imag_part], axis=-1).astype(jnp.bfloat16)
    flat_rows = cross_spec.reshape(-1, cross_spec.shape[-1])
    correlation = jnp.dot(flat_rows, lag_rows, preferred_element_type=jnp.float32) / math.sqrt(
        block_count * half_size
    )
    return correlation.astype(jnp.bfloat16).reshape(
        own_tile.shape[0], sources.shape[0], lag_rows.shape[1]
    )


def owner_slots(segments, segment_row):
    segment_total = segment_row.shape[0]
    matches = segments[:, None] == jnp.arange(segment_total, dtype=jnp.int32)[None, :]
    return jnp.sum(jnp.where(matches, segment_row[None, :], 0), axis=1)


def fill_buckets(values, stack_rows, owners, capacity):
    row_total = values.shape[0]
    owner_ids = stack_rows // SEG_PER
    slot_ids = stack_rows % SEG_PER
    positions = jnp.arange(row_total, dtype=jnp.int32)
    earlier = (owner_ids[:, None] == owner_ids[None, :]) & (positions[:, None] > positions[None, :])
    ranks = jnp.sum(earlier.astype(jnp.int32), axis=1)
    targets = owner_ids * capacity + ranks
    bucket_ids = jnp.arange(owners * capacity, dtype=jnp.int32)
    matches = targets[None, :] == bucket_ids[:, None]
    filled = jnp.any(matches, axis=1)
    picked = jnp.sum(jnp.where(matches, positions[None, :], 0), axis=1)
    buckets = jnp.where(
        filled[:, None, None], jnp.take(values, picked, axis=0), jnp.zeros((), values.dtype)
    )
    labels = jnp.where(filled, jnp.sum(jnp.where(matches, slot_ids[None, :], 0), axis=1), -1)
    return (buckets, labels)


def stack_slots(arrived, labels):
    slot_onehot = (labels[None, :] == jnp.arange(SEG_PER, dtype=jnp.int32)[:, None]).astype(
        jnp.bfloat16
    )
    flat_rows = arrived.reshape(arrived.shape[0], -1)
    summed = jnp.dot(slot_onehot, flat_rows, preferred_element_type=jnp.float32)
    return summed.reshape((SEG_PER,) + arrived.shape[1:])


def slot_counts(channel_segment, segment_row, owner):
    held_rows = owner * SEG_PER + jnp.arange(SEG_PER, dtype=jnp.int32)
    matches = segment_row[None, :] == held_rows[:, None]
    segment_ids = jnp.arange(segment_row.shape[0], dtype=jnp.int32)
    held_segments = jnp.sum(jnp.where(matches, segment_ids[None, :], 0), axis=1)
    members = channel_segment[None, :] == held_segments[:, None]
    return jnp.sum(members.astype(jnp.float32), axis=1)


def on_device(records, window_start, channel_segment, segment_row):
    tile_size = records.shape[0]
    block_count = records.shape[1] // NFFT
    src_count = lax.axis_size("src")
    rcv_count = lax.axis_size("rcv")
    blocks = records.reshape(tile_size * block_count, NFFT)
    spectrum = jnp.dot(
        blocks, dft_table(NFFT), precision=lax.Precision.HIGHEST, preferred_element_type=jnp.float32
    )
    white = whiten(spectrum).astype(jnp.bfloat16).reshape(tile_size, block_count, NFFT)
    gathered = lax.all_gather(white, "src", axis=0, tiled=True)
    position = lax.axis_index("src")
    group_size = gathered.shape[0]
    window_size = group_size // 4
    window_idx = window_start[0] + jnp.arange(window_size, dtype=jnp.int32)
    source_idx = jnp.where(window_idx < position * tile_size, window_idx, window_idx + tile_size)
    sources = jnp.take(gathered, source_idx, axis=0)
    correlation = correlate(white, sources, lag_table(NFFT, LAGS), block_count)
    rcv_index = lax.axis_index("rcv")
    counts = slot_counts(channel_segment, segment_row, rcv_index)
    tile_segments = lax.dynamic_slice_in_dim(
        channel_segment, (rcv_index * src_count + position) * tile_size, tile_size
    )
    buckets, labels = fill_buckets(
        correlation, owner_slots(tile_segments, segment_row), rcv_count, CAP
    )
    arrived, arrived_labels = (
        lax.all_to_all(buckets, "rcv", split_axis=0, concat_axis=0, tiled=True),
        lax.all_to_all(labels, "rcv", split_axis=0, concat_axis=0, tiled=True),
    )
    summed = lax.psum_scatter(
        stack_slots(arrived, arrived_labels), "src", scatter_dimension=1, tiled=True
    )
    return summed / jnp.sqrt(jnp.maximum(counts, 1.0))[:, None, None]


def solution(mesh):
    in_specs = (P(("rcv", "src"), None), P(("rcv", "src")), P(), P())
    out_specs = P("rcv", "src", None)
    return jax.shard_map(
        on_device, mesh=mesh, in_specs=in_specs, out_specs=out_specs, check_vma=False
    )
```

profile of v0, /device:TPU:0, one launch (start us, length us, event | category | flops | bytes accessed | tf_op | source)
XLA Modules:
  0.0 109.0 jit_solution(15245234993975421317)
XLA Ops:
  6.5 0.8 dynamic_slice.3
  7.3 0.8 select_reduce_fusion.2
  8.1 0.2 convert_reduce_fusion.1
  8.3 0.1 fusion.37
  8.5 0.1 select_reduce_fusion.1
  8.6 0.7 select_n.138
  9.3 7.4 %all-to-all-start = ((s32[16,2,1]{1,2,0:T(1,128)}), s32[16,2,1]{1,2,0:T(1,128)}, u32[]{:S(2)}, u32[]{:S(2)}) async-start(s32[16,2,1]{1,2,0:T(1,128)} %bitcast), calls=%async_computation | async-start | bytes 16384 | tf_op jit(solution)/shard_map/all_to_all | solution.py:131
  16.7 9.1 %sine_negate_fusion = (f32[1024,512]{1,0:T(8,128)S(1)}, f32[1024,512]{1,0:T(8,128)}) fusion(), kind=kLoop, calls=%fused_computation.14 | loop fusion | flops 7864320 | bytes 4194304 | tf_op jit(solution)/shard_map/neg | solution.py:20
  25.8 0.1 reshape.164
  26.0 4.0 %fusion.12 = f32[128,1024]{1,0:T(8,128)S(1)} fusion(f32[128,1024]{1,0:T(8,128)S(1)} %reshape.164, f32[1024,512]{1,0:T(8,128)S(1)} %get-tuple-element.13, f32[1024,512]{1,0:T(8,128)} %get-tuple-element.14), kind=kOutput, calls=%fused_computation.21 | convolution fusion | flops 1611661312 | bytes 5242880 | tf_op jit(solution)/shard_map/dot_general | solution.py:109
  30.0 0.1 fusion.36
  30.1 0.2 add_sqrt_fusion
  30.3 0.1 reshape.165
  30.5 9.4 %all_gather.3 = bf16[64,4,1024]{2,1,0:T(4,128)(2,1)S(1)} all-gather(bf16[32,4,1024]{2,1,0:T(4,128)(2,1)S(1)} %reshape.165), channel_id=1, replica_groups=mesh['rcv'=16,'src'=2] {'src'}, dimensions={0}, use_global_device_ids=true | all-gather | bytes 786432 | tf_op jit(solution)/shard_map/all_gather | solution.py:113
  40.7 0.7 gather_fusion
  41.3 0.7 copy.32
  42.1 0.5 broadcast_select_fusion.16
  42.5 1.4 %broadcast_select_fusion.14 = bf16[16,4,1024]{0,1,2:T(4,128)(2,1)} fusion(bf16[16,4,1024]{0,1,2:T(4,128)(2,1)S(1)} %copy.32, pred[16]{0:T(512)(128)(4,1)S(1)} %compare_and_fusion), kind=kLoop, calls=%fused_computation.27.clone.clone.1 | loop fusion | flops 65536 | bytes 262160 | tf_op jit(solution)/shard_map/ibf,jbf->ijf/dot_general | solution.py:46
  44.0 1.5 %broadcast_select_fusion.17 = bf16[16,4,1024]{0,1,2:T(4,128)(2,1)} fusion(bf16[16,4,1024]{0,1,2:T(4,128)(2,1)S(1)} %copy.32, pred[16]{0:T(512)(128)(4,1)S(1)} %compare_and_fusion), kind=kLoop, calls=%fused_computation.27.clone.2.clone.1 | loop fusion | flops 65536 | bytes 262160 | tf_op jit(solution)/shard_map/ibf,jbf->ijf/dot_general | solution.py:46
  45.5 1.4 %broadcast_select_fusion.15 = bf16[16,4,1024]{0,1,2:T(4,128)(2,1)} fusion(bf16[16,4,1024]{0,1,2:T(4,128)(2,1)S(1)} %copy.32, pred[16]{0:T(512)(128)(4,1)S(1)} %compare_and_fusion), kind=kLoop, calls=%fused_computation.27.clone.3.clone.1 | loop fusion | flops 65536 | bytes 262160 | tf_op jit(solution)/shard_map/ibf,jbf->ijf/dot_general | solution.py:46
  46.9 0.5 iota_add_fusion
  47.5 0.5 fusion.43
  48.0 0.5 compare_and_fusion.1
  48.5 0.3 copy.39
  48.8 1.1 copy.40
  49.9 0.8 fusion.30
  50.8 0.4 copy-done.2
  51.1 0.1 copy-done.5
  51.3 1.1 %fusion.10 = bf16[32,16,512]{0,1,2:T(8,128)(2,1)S(1)} fusion(f32[512,16,32]{2,1,0:T(8,128)S(1)} %fusion.30, bf16[32,4,512]{0,1,2:T(4,128)(2,1)S(1)} %copy-done.5, bf16[16,4,1024]{0,1,2:T(4,128)(2,1)S(1)} %copy-done.2), kind=kOutput, calls=%fused_computation.18 | convolution fusion | flops 2621440 | bytes 1835008 | tf_op jit(solution)/shard_map/ibf,jbf->ijf/dot_general | solution.py:46
  52.4 2.9 %copy.35 = bf16[32,16,512]{2,1,0:T(8,128)(2,1)} copy(bf16[32,16,512]{0,1,2:T(8,128)(2,1)S(1)} %fusion.10) | data formatting | bytes 1048576 | tf_op jit(solution)/shard_map/add | solution.py:48
  55.3 2.0 %fusion.31 = f32[512,16,32]{2,1,0:T(8,128)S(1)} fusion(bf16[32,4,512]{0,1,2:T(4,128)(2,1)} %copy-done.4, bf16[16,4,1024]{0,1,2:T(4,128)(2,1)S(1)} %copy-done.1), kind=kOutput, calls=%fused_computation.45 | convolution fusion | flops 2097152 | bytes 1310720 | tf_op jit(solution)/shard_map/ibf,jbf->ijf/dot_general | solution.py:46
  57.3 1.1 %fusion.11 = bf16[32,16,512]{0,1,2:T(8,128)(2,1)S(1)} fusion(f32[512,16,32]{2,1,0:T(8,128)S(1)} %fusion.31, bf16[32,4,512]{0,1,2:T(4,128)(2,1)S(1)} %copy-done.6, bf16[16,4,1024]{0,1,2:T(4,128)(2,1)S(1)} %copy-done), kind=kOutput, calls=%fused_computation.19 | convolution fusion | flops 2621440 | bytes 1835008 | tf_op jit(solution)/shard_map/ibf,jbf->ijf/dot_general | solution.py:46
  58.4 2.2 %copy.36 = bf16[32,16,512]{2,1,0:T(8,128)(2,1)S(1)} copy(bf16[32,16,512]{0,1,2:T(8,128)(2,1)S(1)} %fusion.11) | data formatting | bytes 1048576 | tf_op jit(solution)/shard_map/sub | solution.py:49
  60.6 2.2 %cosine_convert_fusion = (bf16[512,256]{1,0:T(8,128)(2,1)S(1)}, bf16[512,256]{1,0:T(8,128)(2,1)S(1)}) fusion(s32[256]{0:T(256)S(1)} %copy-done.9), kind=kLoop, calls=%fused_computation.40 | loop fusion | flops 2228224 | bytes 525312 | tf_op jit(solution)/shard_map/convert
  62.9 0.4 fusion.15
  63.4 0.6 gather_fusion.1
  64.0 0.8 select_select_fusion
  64.8 5.8 %all-to-all-start.1 = ((bf16[32,16,256]{2,1,0:T(8,128)(2,1)}), bf16[32,16,256]{2,1,0:T(8,128)(2,1)S(1)}, u32[]{:S(2)}, u32[]{:S(2)}) async-start(bf16[32,16,256]{2,1,0:T(8,128)(2,1)} %select_select_fusion), calls=%async_computation.1 | async-start | bytes 524288 | tf_op jit(solution)/shard_map/all_to_all | solution.py:130
  70.7 0.2 select_reduce_fusion.3
  70.8 0.2 convert_reduce_fusion
  71.0 0.5 broadcast.292
  71.5 1.4 %reduce.3 = s32[16,2]{1,0:T(8,128)S(1)} reduce(s32[16,2,1]{1,2,0:T(1,128)} %all-to-all-done, s32[]{:T(128)} %broadcast.292), dimensions={2}, to_apply=%all_to_all.7.reduce_sub_computation.3 | reduce | bytes 260 | tf_op jit(solution)/shard_map/all_to_all | solution.py:131
  73.0 7.6 %all-to-all-done.1 = bf16[32,16,256]{2,1,0:T(8,128)(2,1)S(1)} async-done(((bf16[32,16,256]{2,1,0:T(8,128)(2,1)}), bf16[32,16,256]{2,1,0:T(8,128)(2,1)S(1)}, u32[]{:S(2)}, u32[]{:S(2)}) %all-to-all-start.1) | async-done | bytes 262176 | tf_op jit(solution)/shard_map/all_to_all | solution.py:130
  80.6 0.8 fusion.32
  81.5 0.6 dynamic-slice
  82.7 18.0 %all-reduce.3.cloned.1.call-done = f32[4,16,256]{2,0,1:T(4,128)} async-done(((f32[4,16,256]{2,0,1:T(4,128)}), f32[4,16,256]{2,0,1:T(4,128)}) %all-reduce.3.cloned.1.call-update) | async-done | bytes 65552
  100.7 0.8 constant_dynamic-slice_fusion
  101.5 0.7 copy_divide_fusion
  (46 shorter events, 0.5 us)
Async XLA Ops:
  8.5 0.8 copy-start.11
  9.3 55.5 %all-to-all-start = ((s32[16,2,1]{1,2,0:T(1,128)}), s32[16,2,1]{1,2,0:T(1,128)}, u32[]{:S(2)}, u32[]{:S(2)}) async-start(s32[16,2,1]{1,2,0:T(1,128)} %bitcast), calls=%async_computation | async-start | bytes 16384 | tf_op jit(solution)/shard_map/all_to_all | solution.py:131
  16.7 9.1 %copy-start.7 = (f32[32,4096]{1,0:T(8,128)S(1)}, f32[32,4096]{1,0:T(8,128)}, u32[]{:S(2)}) copy-start(f32[32,4096]{1,0:T(8,128)} %param.4) | copy-start | bytes 1572868
  48.8 1.1 %copy-start.4 = (bf16[32,4,512]{0,1,2:T(4,128)(2,1)}, bf16[32,4,512]{0,1,2:T(4,128)(2,1)S(1)}, u32[]{:S(2)}) copy-start(bf16[32,4,512]{0,1,2:T(4,128)(2,1)S(1)} %copy.39) | copy-start | bytes 393220
  49.9 1.2 %copy-start.2 = (bf16[16,4,1024]{0,1,2:T(4,128)(2,1)S(1)}, bf16[16,4,1024]{0,1,2:T(4,128)(2,1)}, u32[]{:S(2)}) copy-start(bf16[16,4,1024]{0,1,2:T(4,128)(2,1)} %broadcast_select_fusion.14) | copy-start | bytes 393220
  49.9 1.4 %copy-start.5 = (bf16[32,4,512]{0,1,2:T(4,128)(2,1)S(1)}, bf16[32,4,512]{0,1,2:T(4,128)(2,1)}, u32[]{:S(2)}) copy-start(bf16[32,4,512]{0,1,2:T(4,128)(2,1)} %copy.40) | copy-start | bytes 393220
  52.4 2.9 %copy-start.1 = (bf16[16,4,1024]{0,1,2:T(4,128)(2,1)S(1)}, bf16[16,4,1024]{0,1,2:T(4,128)(2,1)}, u32[]{:S(2)}) copy-start(bf16[16,4,1024]{0,1,2:T(4,128)(2,1)} %broadcast_select_fusion.17) | copy-start | bytes 393220
  55.3 2.0 %copy-start = (bf16[16,4,1024]{0,1,2:T(4,128)(2,1)S(1)}, bf16[16,4,1024]{0,1,2:T(4,128)(2,1)}, u32[]{:S(2)}) copy-start(bf16[16,4,1024]{0,1,2:T(4,128)(2,1)} %broadcast_select_fusion.15) | copy-start | bytes 393220
  55.3 2.0 %copy-start.6 = (bf16[32,4,512]{0,1,2:T(4,128)(2,1)S(1)}, bf16[32,4,512]{0,1,2:T(4,128)(2,1)}, u32[]{:S(2)}) copy-start(bf16[32,4,512]{0,1,2:T(4,128)(2,1)} %copy.40) | copy-start | bytes 393220
  58.4 2.2 %copy-start.9 = (s32[256]{0:T(256)S(1)}, s32[256]{0:T(256)}, u32[]{:S(2)}) copy-start(s32[256]{0:T(256)} %iota_add_fusion) | copy-start | bytes 3076
  58.4 4.4 %copy-start.10 = (s32[32]{0:T(128)S(1)}, s32[32]{0:T(128)}, u32[]{:S(2)}) copy-start(s32[32]{0:T(128)} %fusion.43) | copy-start | bytes 388
  58.4 4.5 %copy-start.3 = (bf16[32,16,512]{2,1,0:T(8,128)(2,1)S(1)}, bf16[32,16,512]{2,1,0:T(8,128)(2,1)}, u32[]{:S(2)}) copy-start(bf16[32,16,512]{2,1,0:T(8,128)(2,1)} %copy.35) | copy-start | bytes 1572868
  62.9 1.1 %copy-start.12 = (pred[32]{0:T(512)(128)(4,1)S(1)}, pred[32]{0:T(512)(128)(4,1)}, u32[]{:S(2)}) copy-start(pred[32]{0:T(512)(128)(4,1)} %copy-done.11) | copy-start | bytes 100
  62.9 1.1 %copy-start.13 = (pred[32]{0:T(512)(128)(4,1)S(1)}, pred[32]{0:T(512)(128)(4,1)}, u32[]{:S(2)}) copy-start(pred[32]{0:T(512)(128)(4,1)} %compare_and_fusion.1) | copy-start | bytes 100
  62.9 7.7 %copy-start.14 = (s32[64]{0:T(128)S(1)}, s32[64]{0:T(128)}, u32[]{:S(2)}) copy-start(s32[64]{0:T(128)} %param.7) | copy-start | bytes 772
  62.9 7.9 %copy-start.8 = (s32[1024]{0:T(1024)S(1)}, s32[1024]{0:T(1024)}, u32[]{:S(2)}) copy-start(s32[1024]{0:T(1024)} %param.6) | copy-start | bytes 12292
  62.9 18.6 %copy-start.15 = (u32[32]{0:T(128)S(1)}, u32[32]{0:T(128)}, u32[]{:S(2)}) copy-start(u32[32]{0:T(128)} %constant.120) | copy-start | bytes 388
  64.8 15.8 %all-to-all-start.1 = ((bf16[32,16,256]{2,1,0:T(8,128)(2,1)}), bf16[32,16,256]{2,1,0:T(8,128)(2,1)S(1)}, u32[]{:S(2)}, u32[]{:S(2)}) async-start(bf16[32,16,256]{2,1,0:T(8,128)(2,1)} %select_select_fusion), calls=%async_computation.1 | async-start | bytes 524288 | tf_op jit(solution)/shard_map/all_to_all | solution.py:130
  70.6 30.1 %all-reduce.3.cloned.1.call-start = ((), (), s32[]{:S(2)}) async-start(), calls=%async_computation.2 | async-start | bytes 131072
Sparse Core Ops, SparseCore 0:
  81.6 19.0 all-reduce.2
where the time goes:
time: 110 us; the launch traced here: 109 us
  waiting for transfers between devices  25.6 us (23%)
  other arithmetic  22.6 us (21%)
  between operations  15.1 us (14%)
  starting transfers between devices  13.2 us (12%)
  local copies, waits for them, and re-layouts  12.8 us (12%)
  matrix products  10.3 us (9%)
  blocking collectives  9.42 us (9%)
    unnamed x2, waiting for transfers between devices  18 us
    all_gather x1, blocking collectives, on_device(): gathered = lax.all_gather(white, 'src', axis=0, tiled=True)  9.42 us
    neg x1, other arithmetic, dft_table(): return jnp.concatenate([jnp.cos(angles), -jnp.sin(angles)], axis=1)  9.11 us
    all_to_all x1, waiting for transfers between devices, on_device(): lax.all_to_all(buckets, 'rcv', split_axis=0, concat_axis=0, tiled=True)  7.63 us
    all_to_all x1, starting transfers between devices, on_device(): lax.all_to_all(labels, 'rcv', split_axis=0, concat_axis=0, tiled=True)  7.41 us
    all_to_all x1, starting transfers between devices, on_device(): lax.all_to_all(buckets, 'rcv', split_axis=0, concat_axis=0, tiled=True)  5.75 us
    dot_general x4, matrix products, product(): jnp.einsum('ibf,jbf->ijf', left_part, right_part, preferred_element_type=...  5.04 us
    dot_general x4, other arithmetic, product(): jnp.einsum('ibf,jbf->ijf', left_part, right_part, preferred_element_type=...  4.82 us
  transfers between devices with their start and end apart: 3, of which 2 were waited for; matrix products, arithmetic and copies ran while one was open for 37% of the time, Pallas kernels for 0%

commit v1 on v0

v1 whole, which is shorter than its diff:
```python
import functools
import math

import jax
import jax.numpy as jnp
import ml_dtypes
import numpy as np
from jax import lax
from jax.experimental import pallas as pl
from jax.experimental.pallas import tpu as pltpu
from jax.sharding import PartitionSpec as P

NFFT = 1024
HALF = NFFT // 2
QUART = NFFT // 4
LAGS = 256
CAP = 2
SEG_PER = 4
LANES = 128
OWNERS_STEP = 4
MESH = pl.DeviceIdType.MESH
ORDER = np.concatenate([np.arange(r, HALF, 4) for r in (0, 2, 1, 3)])


def dft_tables():
    parts = []
    for r, rows in ((0, QUART), (2, QUART), (1, 2 * QUART), (3, 2 * QUART)):
        n = np.arange(rows)
        f = np.arange(r, HALF, 4)
        angles = (n[:, None] * f[None, :] % NFFT) * (2.0 * math.pi / NFFT)
        parts.append(np.concatenate([np.cos(angles), -np.sin(angles)], axis=1))
    table = np.concatenate(parts, axis=0).astype(np.float32)
    high = table.astype(ml_dtypes.bfloat16)
    low = (table - high.astype(np.float32)).astype(ml_dtypes.bfloat16)
    return np.stack([high, low])


def lag_table():
    shifts = np.arange(LAGS) - LAGS // 2
    angles = (ORDER[:, None] * shifts[None, :] % NFFT) * (2.0 * math.pi / NFFT)
    table = np.concatenate([np.cos(angles), -np.sin(angles)], axis=0)
    return table.astype(np.float32).astype(ml_dtypes.bfloat16)


def iota(shape, axis):
    return lax.broadcasted_iota(jnp.int32, shape, axis)


def onehot(mask):
    return jnp.where(mask, 1.0, 0.0).astype(jnp.bfloat16)


def mxu(a, b):
    return jnp.dot(a, b, preferred_element_type=jnp.float32)


def kernel(
    rcv_count,
    src_count,
    tile,
    blocks,
    window_start,
    segment_row,
    segments,
    records,
    tables,
    lag_rows,
    out,
    x,
    table,
    lags,
    owner_rows,
    starts_out,
    starts_in,
    white,
    sources_out,
    sources_in,
    own,
    sources,
    cross,
    buckets,
    arrived,
    load_sems,
    start_send,
    start_recv,
    source_send,
    source_recv,
    bucket_send,
    bucket_recv,
):
    rcv = lax.axis_index("rcv")
    pos = lax.axis_index("src")
    me = rcv * src_count + pos
    devices = rcv_count * src_count
    window = tile * src_count // 4
    part = window // src_count
    bucket_rows = rcv_count * CAP
    per_row = LANES // tile
    rows_dest = CAP * part

    loads = [
        pltpu.make_async_copy(records, x, load_sems.at[0]),
        pltpu.make_async_copy(tables, table, load_sems.at[1]),
        pltpu.make_async_copy(lag_rows, lags, load_sems.at[2]),
    ]
    for load in loads:
        load.start()

    barrier = pltpu.get_barrier_semaphore()

    def greet(step, carry):
        other = lax.rem(me + step, devices)
        pl.semaphore_signal(
            barrier,
            inc=1,
            device_id=(other // src_count, lax.rem(other, src_count)),
            device_id_type=MESH,
        )
        return carry

    lax.fori_loop(1, devices, greet, 0)

    starts_out[...] = jnp.full(starts_out.shape, window_start[0], jnp.int32)

    all_segments = segments[...]

    def look_up(segment, rows):
        return rows + jnp.where(all_segments == segment, segment_row[segment], 0)

    stack_rows = lax.fori_loop(
        0, segment_row.shape[0], look_up, jnp.zeros(all_segments.shape, jnp.int32), unroll=8
    )
    owners = stack_rows // SEG_PER
    slots = stack_rows - owners * SEG_PER
    owner_rows[...] = owners
    lane_a, lane_b = iota((LANES, LANES), 0), iota((LANES, LANES), 1)
    earlier = onehot((lane_a // tile == lane_b // tile) & (lane_a < lane_b))

    mine = owners == rcv
    ranks = mxu(onehot(mine), earlier)
    labels = jnp.zeros((owners.shape[0], LANES), jnp.float32)
    for rank in range(CAP):
        value = jnp.where(mine & (ranks == rank), slots + 1, 0).astype(jnp.bfloat16)
        spread = onehot(
            (lane_a // tile == lane_b // rows_dest % per_row) & (lane_b // part % CAP == rank)
        )
        labels = labels + mxu(value, spread)
    arrivals = devices * rows_dest
    labels = jnp.concatenate([labels] * (arrivals // LANES), axis=1)
    row_id = iota(labels.shape, 0)
    lane_id = iota(labels.shape, 1)
    labels = jnp.sum(
        jnp.where(row_id == lane_id // (rows_dest * per_row), labels, 0.0), axis=0, keepdims=True
    )
    out_id = iota((SEG_PER * part, arrivals), 0)
    lane_id = iota((SEG_PER * part, arrivals), 1)
    chosen = (labels == (out_id // part + 1).astype(jnp.float32)) & (
        out_id % part == lane_id % part
    )
    summing = jnp.where(chosen, 1.0, 0.0)
    counts = jnp.sum(summing, axis=1, keepdims=True)
    out_scale = 1.0 / jnp.sqrt(jnp.maximum(counts, 1.0))
    summing = summing.astype(jnp.bfloat16)

    tile_owners = owner_rows[pl.ds(me // per_row, 1), :]
    bucket_id = iota((bucket_rows, LANES), 0)
    held = bucket_id // CAP == tile_owners
    tile_ranks = mxu(onehot(held), earlier)
    placed = onehot(held & (tile_ranks == (bucket_id % CAP).astype(jnp.float32)))
    fold = onehot(
        (lane_a // tile == lax.rem(me, per_row)) & (lane_a % tile == lane_b % tile)
    )
    placed = mxu(placed, fold)
    placed = jnp.concatenate([placed] * blocks, axis=0)
    placed = jnp.where(
        iota(placed.shape, 0) // bucket_rows == iota(placed.shape, 1) // tile, placed, 0.0
    ).astype(jnp.bfloat16)

    pl.semaphore_wait(barrier, devices - 1)

    def start_copy(step):
        other = lax.rem(pos + step, src_count)
        return pltpu.make_async_remote_copy(
            src_ref=starts_out,
            dst_ref=starts_in.at[step - 1],
            send_sem=start_send.at[step - 1],
            recv_sem=start_recv.at[step - 1],
            device_id=(rcv, other),
            device_id_type=MESH,
        )

    for step in range(1, src_count):
        start_copy(step).start()

    loads[0].wait()
    quarters = []
    for quarter in range(4):
        quarters.append(
            jnp.concatenate(
                [
                    x[:, block * NFFT + quarter * QUART : block * NFFT + (quarter + 1) * QUART]
                    for block in range(blocks)
                ],
                axis=0,
            )
        )
    even_a, even_b = quarters[0] + quarters[2], quarters[1] + quarters[3]
    odd = jnp.concatenate([quarters[0] - quarters[2], quarters[1] - quarters[3]], axis=1)
    inputs = [even_a + even_b, even_a - even_b, odd, odd]
    loads[1].wait()
    height = blocks * tile
    real_parts, imag_parts = [], []
    first = 0
    for values in inputs:
        depth = values.shape[1]
        high = values.astype(jnp.bfloat16)
        low = (values - high.astype(jnp.float32)).astype(jnp.bfloat16)
        both = mxu(jnp.concatenate([high, low], axis=0), table[0, first : first + depth, :])
        total = both[:height] + both[height:] + mxu(high, table[1, first : first + depth, :])
        first += depth
        real_parts.append(total[:, :LANES])
        imag_parts.append(total[:, LANES:])
    real = jnp.concatenate(real_parts, axis=1)
    imag = jnp.concatenate(imag_parts, axis=1)
    powers = real * real + imag * imag
    mean_power = jnp.mean(powers, axis=1, keepdims=True)
    factor = lax.rsqrt(powers + 0.1 * mean_power + 1e-06)
    white[...] = jnp.concatenate([real * factor, imag * factor], axis=1).astype(jnp.bfloat16)

    def source_copy(step):
        other = lax.rem(pos + step, src_count)
        return pltpu.make_async_remote_copy(
            src_ref=sources_out.at[step - 1],
            dst_ref=sources_in.at[step - 1],
            send_sem=source_send.at[step - 1],
            recv_sem=source_recv.at[step - 1],
            device_id=(rcv, other),
            device_id_type=MESH,
        )

    for step in range(1, src_count):
        other = lax.rem(pos + step, src_count)
        start_copy(src_count - step).wait_recv()
        first_position = starts_in[src_count - step - 1, 0:1, :]
        my_place = pos - jnp.where(pos < other, 0, 1)
        row_id = iota((blocks * window, LANES), 0)
        lane_id = iota((blocks * window, LANES), 1)
        asked = (first_position + row_id % window == my_place * tile + lane_id % tile) & (
            row_id // window == lane_id // tile
        )
        sources_out[step - 1] = mxu(onehot(asked), white[...]).astype(jnp.bfloat16)
        source_copy(step).start()

    own[...] = mxu(placed, white[...])

    loads[2].wait()
    for step in range(1, src_count):
        source_copy(step).wait_recv()
    total = sources_in[0].astype(jnp.float32)
    for step in range(2, src_count):
        total = total + sources_in[step - 1].astype(jnp.float32)
    sources[...] = total

    scale = 1.0 / math.sqrt(blocks * HALF)
    steps = rcv_count // OWNERS_STEP
    group_rows = src_count * rows_dest

    def bucket_copy(owner, place):
        return pltpu.make_async_remote_copy(
            src_ref=buckets.at[owner * src_count + place],
            dst_ref=arrived.at[me],
            send_sem=bucket_send,
            recv_sem=bucket_recv,
            device_id=(owner, place),
            device_id_type=MESH,
        )

    def owner_step(step, carry):
        chunk = lax.rem(rcv // OWNERS_STEP + 1 + step, steps)

        def cross_step(index, inner):
            re_cols = pl.ds(pl.multiple_of(index * LANES, LANES), LANES)
            im_cols = pl.ds(pl.multiple_of(HALF + index * LANES, LANES), LANES)
            group = OWNERS_STEP * CAP
            left = []
            for block in range(blocks):
                first_row = pl.multiple_of(block * bucket_rows + chunk * group, group)
                rows = pl.ds(first_row, group)
                left.append((own[rows, re_cols], own[rows, im_cols]))
            for place in range(src_count):
                right = []
                for block in range(blocks):
                    rows = slice(block * window + place * part, block * window + (place + 1) * part)
                    right.append((sources[rows, re_cols], sources[rows, im_cols]))
                for owner in range(OWNERS_STEP):
                    reals, imags = [], []
                    for rank in range(CAP):
                        row = slice(owner * CAP + rank, owner * CAP + rank + 1)
                        re_sum, im_sum = None, None
                        for block in range(blocks):
                            left_re, left_im = left[block][0][row], left[block][1][row]
                            right_re, right_im = right[block]
                            re_term = left_re * right_re + left_im * right_im
                            im_term = left_re * right_im - left_im * right_re
                            re_sum = re_term if re_sum is None else re_sum + re_term
                            im_sum = im_term if im_sum is None else im_sum + im_term
                        reals.append(re_sum)
                        imags.append(im_sum)
                    at = owner * group_rows + place * rows_dest
                    rows = slice(at, at + rows_dest)
                    cross[rows, re_cols] = jnp.concatenate(reals, axis=0).astype(jnp.bfloat16)
                    cross[rows, im_cols] = jnp.concatenate(imags, axis=0).astype(jnp.bfloat16)
            return inner

        lax.fori_loop(0, HALF // LANES, cross_step, 0)
        rows = (mxu(cross[...], lags[...]) * scale).astype(jnp.bfloat16)
        dests = OWNERS_STEP * src_count
        buckets[pl.ds(chunk * dests, dests)] = rows.reshape(dests, rows_dest, LAGS)

        def send(index, inner):
            dest = chunk * dests + index

            @pl.when(dest != me)
            def _():
                bucket_copy(dest // src_count, lax.rem(dest, src_count)).start()

            return inner

        lax.fori_loop(0, dests, send, 0)
        return carry

    lax.fori_loop(0, steps, owner_step, 0)
    arrived[pl.ds(me, 1)] = buckets[pl.ds(me, 1)]

    others = pl.ds(0, devices - 1)
    pltpu.make_async_copy(arrived.at[others], arrived.at[others], bucket_recv).wait()
    stacked = mxu(summing, arrived[...].reshape(arrivals, LAGS)) * out_scale
    out[...] = stacked.reshape(SEG_PER, part, LAGS)

    pltpu.make_async_copy(buckets.at[others], buckets.at[others], bucket_send).wait()
    for step in range(1, src_count):
        start_copy(step).wait_send()
        source_copy(step).wait_send()


def on_device(rcv_count, src_count, records, window_start, channel_segment, segment_row):
    tile, samples = records.shape
    blocks = samples // NFFT
    devices = rcv_count * src_count
    window = tile * src_count // 4
    part = window // src_count
    rows_dest = CAP * part
    bucket_rows = rcv_count * CAP
    segments = channel_segment.reshape(-1, LANES)
    tables = jnp.asarray(dft_tables())
    lag_rows = jnp.asarray(lag_table())
    smem = pl.BlockSpec(memory_space=pltpu.SMEM)
    vmem = pl.BlockSpec(memory_space=pltpu.VMEM)
    anywhere = pl.BlockSpec(memory_space=pl.ANY)
    bf16, f32, i32 = jnp.bfloat16, jnp.float32, jnp.int32
    dma = pltpu.SemaphoreType.DMA
    return pl.pallas_call(
        functools.partial(kernel, rcv_count, src_count, tile, blocks),
        out_shape=jax.ShapeDtypeStruct((SEG_PER, part, LAGS), f32),
        in_specs=[smem, smem, vmem, anywhere, anywhere, anywhere],
        out_specs=vmem,
        scratch_shapes=[
            pltpu.VMEM(records.shape, f32),
            pltpu.VMEM(tables.shape, bf16),
            pltpu.VMEM(lag_rows.shape, bf16),
            pltpu.VMEM(segments.shape, i32),
            pltpu.VMEM((8, LANES), i32),
            pltpu.VMEM((src_count - 1, 8, LANES), i32),
            pltpu.VMEM((blocks * tile, NFFT), bf16),
            pltpu.VMEM((src_count - 1, blocks * window, NFFT), bf16),
            pltpu.VMEM((src_count - 1, blocks * window, NFFT), bf16),
            pltpu.VMEM((blocks * bucket_rows, NFFT), f32),
            pltpu.VMEM((blocks * window, NFFT), f32),
            pltpu.VMEM((OWNERS_STEP * src_count * rows_dest, NFFT), bf16),
            pltpu.VMEM((devices, rows_dest, LAGS), bf16),
            pltpu.VMEM((devices, rows_dest, LAGS), bf16),
            dma((3,)),
            dma((src_count - 1,)),
            dma((src_count - 1,)),
            dma((src_count - 1,)),
            dma((src_count - 1,)),
            dma,
            dma,
        ],
        compiler_params=pltpu.CompilerParams(
            collective_id=0, has_side_effects=True, vmem_limit_bytes=48 * 1024 * 1024
        ),
    )(window_start, segment_row, segments, records, tables, lag_rows)


def solution(mesh):
    in_specs = (P(("rcv", "src"), None), P(("rcv", "src")), P(), P())
    out_specs = P("rcv", "src", None)
    return jax.shard_map(
        functools.partial(on_device, mesh.shape["rcv"], mesh.shape["src"]),
        mesh=mesh,
        in_specs=in_specs,
        out_specs=out_specs,
        check_vma=False,
    )
```

time: 110 us -> 26.5 us (0.24)
  waiting for transfers between devices: 25.6 us -> 0 us
  other arithmetic: 22.6 us -> 0 us
  Pallas kernels: 0 us -> 20.1 us
  between operations: 15.1 us -> 0.67 us
  starting transfers between devices: 13.2 us -> 0 us
  matrix products: 10.3 us -> 0 us
  blocking collectives: 9.42 us -> 0 us
  local copies, waits for them, and re-layouts: 12.8 us -> 5.44 us
    pallas_call x0 -> x1, Pallas kernels: none -> 20.1 us  [on_device(): pl.pallas_call(functools.partial(kernel, rcv_count, src_count, tile, bloc...]
    unnamed x2 -> x0, waiting for transfers between devices: 18 us -> none
    all_to_all x2 -> x0, starting transfers between devices: 13.2 us -> none  [the longest x1 7.41 us: on_device(): lax.all_to_all(labels, 'rcv', split_axis=0, concat_axis=0, tiled=True)]
    dot_general x7 -> x0, matrix products: 10.3 us -> none  [the longest x4 5.04 us: product(): jnp.einsum('ibf,jbf->ijf', left_part, right_part, preferred_element_type=...]
    all_gather x1 -> x0, blocking collectives: 9.42 us -> none  [on_device(): gathered = lax.all_gather(white, 'src', axis=0, tiled=True)]
    neg x1 -> x0, other arithmetic: 9.11 us -> none  [dft_table(): return jnp.concatenate([jnp.cos(angles), -jnp.sin(angles)], axis=1)]
    all_to_all x2 -> x0, waiting for transfers between devices: 7.63 us -> none  [the longest x1 7.63 us: on_device(): lax.all_to_all(buckets, 'rcv', split_axis=0, concat_axis=0, tiled=True)]
    dot_general x4 -> x0, other arithmetic: 4.82 us -> none  [product(): jnp.einsum('ibf,jbf->ijf', left_part, right_part, preferred_element_type=...]
  transfers between devices with their start and end apart: 3 -> 0, of which waited for: 2 -> 0; matrix products, arithmetic and copies ran while one was open for 37% -> 0% of each run, Pallas kernels for 0% -> 0%
where the time goes in v1:
time: 26.5 us; the launch traced here: 26.2 us
  Pallas kernels  20.1 us (76%)
  local copies, waits for them, and re-layouts  5.44 us (21%)
  between operations  0.67 us (3%)
    pallas_call x1, Pallas kernels, on_device(): pl.pallas_call(functools.partial(kernel, rcv_count, src_count, tile, bloc...  20.1 us
    unnamed x11, local copies, waits for them, and re-layouts  5.44 us

profile of v1, /device:TPU:0, one launch (start us, length us, event | category | flops | bytes accessed | tf_op | source)
XLA Modules:
  0.0 26.2 jit_solution(16652961627241497480)
XLA Ops:
  0.7 0.0 copy-start
  0.7 1.4 %copy-done = bf16[2,1536,256]{2,1,0:T(8,128)(2,1)S(1)} copy-done((bf16[2,1536,256]{2,1,0:T(8,128)(2,1)S(1)}, bf16[2,1536,256]{2,1,0:T(8,128)(2,1)}, u32[]{:S(2)}) %copy-start) | copy-done | bytes 1572888
  2.1 0.0 copy-start.1
  2.1 1.0 %copy-done.1 = f32[32,4096]{1,0:T(8,128)S(1)} copy-done((f32[32,4096]{1,0:T(8,128)S(1)}, f32[32,4096]{1,0:T(8,128)}, u32[]{:S(2)}) %copy-start.1) | copy-done | bytes 524312
  3.1 0.0 copy-start.2
  3.1 1.0 %copy-done.2 = bf16[1024,256]{1,0:T(8,128)(2,1)S(1)} copy-done((bf16[1024,256]{1,0:T(8,128)(2,1)S(1)}, bf16[1024,256]{1,0:T(8,128)(2,1)}, u32[]{:S(2)}) %copy-start.2) | copy-done | bytes 524312
  4.1 0.0 copy-start.3
  4.2 0.7 %copy-done.3 = s32[1024]{0:T(1024)S(1)} copy-done((s32[1024]{0:T(1024)S(1)}, s32[1024]{0:T(1024)}, u32[]{:S(2)}) %copy-start.3) | copy-done | bytes 4120
  4.8 0.0 copy-start.4
  4.8 0.7 %copy-done.4 = s32[64]{0:T(128)S(1)} copy-done((s32[64]{0:T(128)S(1)}, s32[64]{0:T(128)}, u32[]{:S(2)}) %copy-start.4) | copy-done | bytes 280
  5.5 20.1 %shard_map.64 = f32[4,8,256]{2,1,0:T(8,128)S(1)} custom-call(s32[1]{0:T(128)S(6)} %copy.8.window_start, s32[64]{0:T(128)S(1)} %copy-done.4, s32[8,128]{1,0:T(8,128)S(1)} %bitcast.1, f32[32,4096]{1,0:T(8,128)S(1)} %copy-done.1, bf16[2,1536,256]{2,1,0:T(8,128)(2,1)S(1)} %copy-done, bf16[1024,256]{1,0:T(8,128)(2,1)S(1)} %copy-done.2), custom_call_target="tpu_custom_call" | custom-call | tf_op jit(solution)/shard_map/pallas_call | solution.py:362
  25.6 0.6 %copy.9 = f32[4,8,256]{2,1,0:T(8,128)} copy(f32[4,8,256]{2,1,0:T(8,128)S(1)} %shard_map.64) | data formatting | bytes 65536
Async XLA Ops:
  0.7 1.4 %copy-start = (bf16[2,1536,256]{2,1,0:T(8,128)(2,1)S(1)}, bf16[2,1536,256]{2,1,0:T(8,128)(2,1)}, u32[]{:S(2)}) copy-start(bf16[2,1536,256]{2,1,0:T(8,128)(2,1)} %constant.4.clone.tables) | copy-start | bytes 4718596
  2.1 1.0 %copy-start.1 = (f32[32,4096]{1,0:T(8,128)S(1)}, f32[32,4096]{1,0:T(8,128)}, u32[]{:S(2)}) copy-start(f32[32,4096]{1,0:T(8,128)} %records.1) | copy-start | bytes 1572868
  3.1 1.0 %copy-start.2 = (bf16[1024,256]{1,0:T(8,128)(2,1)S(1)}, bf16[1024,256]{1,0:T(8,128)(2,1)}, u32[]{:S(2)}) copy-start(bf16[1024,256]{1,0:T(8,128)(2,1)} %constant.5.clone.lag_rows) | copy-start | bytes 1572868
  4.1 0.7 %copy-start.3 = (s32[1024]{0:T(1024)S(1)}, s32[1024]{0:T(1024)}, u32[]{:S(2)}) copy-start(s32[1024]{0:T(1024)} %param.8) | copy-start | bytes 12292
  4.8 0.7 %copy-start.4 = (s32[64]{0:T(128)S(1)}, s32[64]{0:T(128)}, u32[]{:S(2)}) copy-start(s32[64]{0:T(128)} %segment_row.1) | copy-start | bytes 772

commit v2 on v1

--- a/solution.py
+++ b/solution.py
@@ -60,12 +60,14 @@
     tile,
     blocks,
     window_start,
-    segment_row,
-    segments,
+    segment_row_in,
+    segments_in,
     records,
     tables,
     lag_rows,
     out,
+    segment_row,
+    segments,
     x,
     table,
     lags,
@@ -101,7 +103,9 @@
     loads = [
         pltpu.make_async_copy(records, x, load_sems.at[0]),
         pltpu.make_async_copy(tables, table, load_sems.at[1]),
-        pltpu.make_async_copy(lag_rows, lags, load_sems.at[2]),
+        pltpu.make_async_copy(segments_in, segments, load_sems.at[2]),
+        pltpu.make_async_copy(segment_row_in, segment_row, load_sems.at[3]),
+        pltpu.make_async_copy(lag_rows, lags, load_sems.at[4]),
     ]
     for load in loads:
         load.start()
@@ -122,60 +126,7 @@
 
     starts_out[...] = jnp.full(starts_out.shape, window_start[0], jnp.int32)
 
-    all_segments = segments[...]
-
-    def look_up(segment, rows):
-        return rows + jnp.where(all_segments == segment, segment_row[segment], 0)
-
-    stack_rows = lax.fori_loop(
-        0, segment_row.shape[0], look_up, jnp.zeros(all_segments.shape, jnp.int32), unroll=8
-    )
-    owners = stack_rows // SEG_PER
-    slots = stack_rows - owners * SEG_PER
-    owner_rows[...] = owners
-    lane_a, lane_b = iota((LANES, LANES), 0), iota((LANES, LANES), 1)
-    earlier = onehot((lane_a // tile == lane_b // tile) & (lane_a < lane_b))
-
-    mine = owners == rcv
-    ranks = mxu(onehot(mine), earlier)
-    labels = jnp.zeros((owners.shape[0], LANES), jnp.float32)
-    for rank in range(CAP):
-        value = jnp.where(mine & (ranks == rank), slots + 1, 0).astype(jnp.bfloat16)
-        spread = onehot(
-            (lane_a // tile == lane_b // rows_dest % per_row) & (lane_b // part % CAP == rank)
-        )
-        labels = labels + mxu(value, spread)
-    arrivals = devices * rows_dest
-    labels = jnp.concatenate([labels] * (arrivals // LANES), axis=1)
-    row_id = iota(labels.shape, 0)
-    lane_id = iota(labels.shape, 1)
-    labels = jnp.sum(
-        jnp.where(row_id == lane_id // (rows_dest * per_row), labels, 0.0), axis=0, keepdims=True
-    )
-    out_id = iota((SEG_PER * part, arrivals), 0)
-    lane_id = iota((SEG_PER * part, arrivals), 1)
-    chosen = (labels == (out_id // part + 1).astype(jnp.float32)) & (
-        out_id % part == lane_id % part
-    )
-    summing = jnp.where(chosen, 1.0, 0.0)
-    counts = jnp.sum(summing, axis=1, keepdims=True)
-    out_scale = 1.0 / jnp.sqrt(jnp.maximum(counts, 1.0))
-    summing = summing.astype(jnp.bfloat16)
-
-    tile_owners = owner_rows[pl.ds(me // per_row, 1), :]
-    bucket_id = iota((bucket_rows, LANES), 0)
-    held = bucket_id // CAP == tile_owners
-    tile_ranks = mxu(onehot(held), earlier)
-    placed = onehot(held & (tile_ranks == (bucket_id % CAP).astype(jnp.float32)))
-    fold = onehot(
-        (lane_a // tile == lax.rem(me, per_row)) & (lane_a % tile == lane_b % tile)
-    )
-    placed = mxu(placed, fold)
-    placed = jnp.concatenate([placed] * blocks, axis=0)
-    placed = jnp.where(
-        iota(placed.shape, 0) // bucket_rows == iota(placed.shape, 1) // tile, placed, 0.0
-    ).astype(jnp.bfloat16)
-
+    loads[0].wait()
     pl.semaphore_wait(barrier, devices - 1)
 
     def start_copy(step):
@@ -192,7 +143,6 @@
     for step in range(1, src_count):
         start_copy(step).start()
 
-    loads[0].wait()
     quarters = []
     for quarter in range(4):
         quarters.append(
@@ -251,9 +201,65 @@
         sources_out[step - 1] = mxu(onehot(asked), white[...]).astype(jnp.bfloat16)
         source_copy(step).start()
 
+    loads[2].wait()
+    loads[3].wait()
+    all_segments = segments[...]
+
+    def look_up(segment, rows):
+        return rows + jnp.where(all_segments == segment, segment_row[segment], 0)
+
+    stack_rows = lax.fori_loop(
+        0, segment_row.shape[0], look_up, jnp.zeros(all_segments.shape, jnp.int32), unroll=8
+    )
+    owners = stack_rows // SEG_PER
+    slots = stack_rows - owners * SEG_PER
+    owner_rows[...] = owners
+    lane_a, lane_b = iota((LANES, LANES), 0), iota((LANES, LANES), 1)
+    earlier = onehot((lane_a // tile == lane_b // tile) & (lane_a < lane_b))
+
+    mine = owners == rcv
+    ranks = mxu(onehot(mine), earlier)
+    labels = jnp.zeros((owners.shape[0], LANES), jnp.float32)
+    for rank in range(CAP):
+        value = jnp.where(mine & (ranks == rank), slots + 1, 0).astype(jnp.bfloat16)
+        spread = onehot(
+            (lane_a // tile == lane_b // rows_dest % per_row) & (lane_b // part % CAP == rank)
+        )
+        labels = labels + mxu(value, spread)
+    arrivals = devices * rows_dest
+    labels = jnp.concatenate([labels] * (arrivals // LANES), axis=1)
+    row_id = iota(labels.shape, 0)
+    lane_id = iota(labels.shape, 1)
+    labels = jnp.sum(
+        jnp.where(row_id == lane_id // (rows_dest * per_row), labels, 0.0), axis=0, keepdims=True
+    )
+    out_id = iota((SEG_PER * part, arrivals), 0)
+    lane_id = iota((SEG_PER * part, arrivals), 1)
+    chosen = (labels == (out_id // part + 1).astype(jnp.float32)) & (
+        out_id % part == lane_id % part
+    )
+    summing = jnp.where(chosen, 1.0, 0.0)
+    counts = jnp.sum(summing, axis=1, keepdims=True)
+    out_scale = 1.0 / jnp.sqrt(jnp.maximum(counts, 1.0))
+    summing = summing.astype(jnp.bfloat16)
+
+    tile_owners = owner_rows[pl.ds(me // per_row, 1), :]
+    bucket_id = iota((bucket_rows, LANES), 0)
+    held = bucket_id // CAP == tile_owners
+    tile_ranks = mxu(onehot(held), earlier)
+    placed = onehot(held & (tile_ranks == (bucket_id % CAP).astype(jnp.float32)))
+    fold = onehot(
+        (lane_a // tile == lax.rem(me, per_row)) & (lane_a % tile == lane_b % tile)
+    )
+    placed = mxu(placed, fold)
+    placed = jnp.concatenate([placed] * blocks, axis=0)
+    placed = jnp.where(
+        iota(placed.shape, 0) // bucket_rows == iota(placed.shape, 1) // tile, placed, 0.0
+    ).astype(jnp.bfloat16)
+
     own[...] = mxu(placed, white[...])
 
-    loads[2].wait()
+    loads[4].wait()
     for step in range(1, src_count):
         source_copy(step).wait_recv()
     total = sources_in[0].astype(jnp.float32)
@@ -356,15 +362,17 @@
     lag_rows = jnp.asarray(lag_table())
     smem = pl.BlockSpec(memory_space=pltpu.SMEM)
     vmem = pl.BlockSpec(memory_space=pltpu.VMEM)
-    anywhere = pl.BlockSpec(memory_space=pl.ANY)
+    hbm = pl.BlockSpec(memory_space=pltpu.HBM)
     bf16, f32, i32 = jnp.bfloat16, jnp.float32, jnp.int32
     dma = pltpu.SemaphoreType.DMA
     return pl.pallas_call(
         functools.partial(kernel, rcv_count, src_count, tile, blocks),
         out_shape=jax.ShapeDtypeStruct((SEG_PER, part, LAGS), f32),
-        in_specs=[smem, smem, vmem, anywhere, anywhere, anywhere],
+        in_specs=[smem, hbm, hbm, hbm, hbm, hbm],
         out_specs=vmem,
         scratch_shapes=[
+            pltpu.SMEM(segment_row.shape, i32),
+            pltpu.VMEM(segments.shape, i32),
             pltpu.VMEM(records.shape, f32),
             pltpu.VMEM(tables.shape, bf16),
             pltpu.VMEM(lag_rows.shape, bf16),
@@ -379,7 +387,7 @@
             pltpu.VMEM((OWNERS_STEP * src_count * rows_dest, NFFT), bf16),
             pltpu.VMEM((devices, rows_dest, LAGS), bf16),
             pltpu.VMEM((devices, rows_dest, LAGS), bf16),
-            dma((3,)),
+            dma((5,)),
             dma((src_count - 1,)),
             dma((src_count - 1,)),
             dma((src_count - 1,)),
@@ -388,7 +396,7 @@
             dma,
         ],
         compiler_params=pltpu.CompilerParams(
-            collective_id=0, has_side_effects=True, vmem_limit_bytes=48 * 1024 * 1024
+            collective_id=0, has_side_effects=True, vmem_limit_bytes=62 * 1024 * 1024
         ),
     )(window_start, segment_row, segments, records, tables, lag_rows)
 

time: 26.5 us -> 22.3 us (0.84)
  local copies, waits for them, and re-layouts: 5.44 us -> 1.38 us
    unnamed x11 -> x1, local copies, waits for them, and re-layouts: 5.44 us -> 1.38 us
where the time goes in v2:
time: 22.3 us; the launch traced here: 22.1 us
  Pallas kernels  20 us (90%)
  local copies, waits for them, and re-layouts  1.38 us (6%)
  between operations  0.66 us (3%)
    pallas_call x1, Pallas kernels, on_device(): pl.pallas_call(functools.partial(kernel, rcv_count, src_count, tile, bloc...  20 us
    unnamed x1, local copies, waits for them, and re-layouts  1.38 us

profile of v2, /device:TPU:0, one launch (start us, length us, event | category | flops | bytes accessed | tf_op | source)
XLA Modules:
  0.0 22.1 jit_solution(16174861008130090560)
XLA Ops:
  0.7 20.0 %shard_map.64 = f32[4,8,256]{2,1,0:T(8,128)} custom-call(s32[1]{0:T(128)S(6)} %copy.8.window_start, s32[64]{0:T(128)} %segment_row_in.1, s32[8,128]{1,0:T(8,128)} %bitcast.1, f32[32,4096]{1,0:T(8,128)} %records.1, bf16[2,1536,256]{2,1,0:T(8,128)(2,1)} %constant.4.clone.tables, bf16[1024,256]{1,0:T(8,128)(2,1)} %constant.5.clone.lag_rows), custom_call_target="tpu_custom_call" | custom-call | tf_op jit(solution)/shard_map/pallas_call | solution.py:368
  20.7 1.4 %copy.9 = f32[4,8,256]{2,1,0:T(8,128)} copy(f32[4,8,256]{2,1,0:T(8,128)} %shard_map.64) | data formatting | bytes 65536

commit v3 on v2

--- a/solution.py
+++ b/solution.py
@@ -18,6 +18,7 @@
 SEG_PER = 4
 LANES = 128
 OWNERS_STEP = 4
+DELAY = 2
 MESH = pl.DeviceIdType.MESH
 ORDER = np.concatenate([np.arange(r, HALF, 4) for r in (0, 2, 1, 3)])
 
@@ -44,6 +45,14 @@
 
 def iota(shape, axis):
     return lax.broadcasted_iota(jnp.int32, shape, axis)
+
+
+def div(a, b):
+    return lax.shift_right_logical(a, b.bit_length() - 1) if b & (b - 1) == 0 else a // b
+
+
+def mod(a, b):
+    return a & (b - 1) if b & (b - 1) == 0 else a % b
 
 
 def onehot(mask):
@@ -72,6 +81,7 @@
     table,
     lags,
     owner_rows,
+    summing,
     starts_out,
     starts_in,
     white,
@@ -82,6 +92,8 @@
     cross,
     buckets,
     arrived,
+    partial,
+    arrived_sums,
     load_sems,
     start_send,
     start_recv,
@@ -89,11 +101,12 @@
     source_recv,
     bucket_send,
     bucket_recv,
+    sum_send,
+    sum_recv,
 ):
     rcv = lax.axis_index("rcv")
     pos = lax.axis_index("src")
     me = rcv * src_count + pos
-    devices = rcv_count * src_count
     window = tile * src_count // 4
     part = window // src_count
     bucket_rows = rcv_count * CAP
@@ -112,22 +125,37 @@
 
     barrier = pltpu.get_barrier_semaphore()
 
-    def greet(step, carry):
-        other = lax.rem(me + step, devices)
+    steps = rcv_count // OWNERS_STEP
+    plane_size = OWNERS_STEP * src_count
+    plane = div(rcv, OWNERS_STEP)
+    spot = lax.rem(me, plane_size)
+
+    def signal(plane_id, spot_id):
         pl.semaphore_signal(
             barrier,
             inc=1,
-            device_id=(other // src_count, lax.rem(other, src_count)),
+            device_id=(
+                plane_id * OWNERS_STEP + spot_id // src_count,
+                lax.rem(spot_id, src_count),
+            ),
             device_id_type=MESH,
         )
+
+    def greet_plane(step, carry):
+        signal(plane, lax.rem(spot + step, plane_size))
         return carry
 
-    lax.fori_loop(1, devices, greet, 0)
+    def greet_planes(step, carry):
+        signal(lax.rem(plane + step, steps), spot)
+        return carry
+
+    lax.fori_loop(1, plane_size, greet_plane, 0)
+    lax.fori_loop(1, steps, greet_planes, 0)
 
     starts_out[...] = jnp.full(starts_out.shape, window_start[0], jnp.int32)
 
     loads[0].wait()
-    pl.semaphore_wait(barrier, devices - 1)
+    pl.semaphore_wait(barrier, plane_size + steps - 2)
 
     def start_copy(step):
         other = lax.rem(pos + step, src_count)
@@ -195,8 +223,8 @@
         my_place = pos - jnp.where(pos < other, 0, 1)
         row_id = iota((blocks * window, LANES), 0)
         lane_id = iota((blocks * window, LANES), 1)
-        asked = (first_position + row_id % window == my_place * tile + lane_id % tile) & (
-            row_id // window == lane_id // tile
+        asked = (first_position + mod(row_id, window) == my_place * tile + mod(lane_id, tile)) & (
+            div(row_id, window) == div(lane_id, tile)
         )
         sources_out[step - 1] = mxu(onehot(asked), white[...]).astype(jnp.bfloat16)
         source_copy(step).start()
@@ -211,50 +239,63 @@
     stack_rows = lax.fori_loop(
         0, segment_row.shape[0], look_up, jnp.zeros(all_segments.shape, jnp.int32), unroll=8
     )
-    owners = stack_rows // SEG_PER
-    slots = stack_rows - owners * SEG_PER
+    owners = div(stack_rows, SEG_PER)
+    slots = mod(stack_rows, SEG_PER)
     owner_rows[...] = owners
     lane_a, lane_b = iota((LANES, LANES), 0), iota((LANES, LANES), 1)
-    earlier = onehot((lane_a // tile == lane_b // tile) & (lane_a < lane_b))
-
-    mine = owners == rcv
+    earlier = onehot((div(lane_a, tile) == div(lane_b, tile)) & (lane_a < lane_b))
+
+    out_rows = SEG_PER * part
+    out_id = iota((out_rows, 1), 0)
+    counts = jnp.zeros((out_rows, 1), jnp.float32)
+    for slot in range(SEG_PER):
+        members = jnp.where(stack_rows == rcv * SEG_PER + slot, 1.0, 0.0)
+        members = jnp.sum(jnp.sum(members, axis=0, keepdims=True), axis=1, keepdims=True)
+        counts = counts + jnp.where(div(out_id, part) == slot, members, 0.0)
+    out_scale = 1.0 / jnp.sqrt(jnp.maximum(counts, 1.0))
+
+    plane_lanes = plane_size * rows_dest
+    row_count = owners.shape[0]
+    owner_here = lax.rem(rcv, OWNERS_STEP)
+    mine = jnp.concatenate(
+        [owners == step * OWNERS_STEP + owner_here for step in range(steps)], axis=0
+    )
+    all_slots = jnp.concatenate([slots] * steps, axis=0)
     ranks = mxu(onehot(mine), earlier)
-    labels = jnp.zeros((owners.shape[0], LANES), jnp.float32)
+    labels = jnp.zeros(mine.shape, jnp.float32)
     for rank in range(CAP):
-        value = jnp.where(mine & (ranks == rank), slots + 1, 0).astype(jnp.bfloat16)
+        value = jnp.where(mine & (ranks == rank), all_slots + 1, 0).astype(jnp.bfloat16)
         spread = onehot(
-            (lane_a // tile == lane_b // rows_dest % per_row) & (lane_b // part % CAP == rank)
+            (div(lane_a, tile) == mod(div(lane_b, rows_dest), per_row))
+            & (mod(div(lane_b, part), CAP) == rank)
         )
         labels = labels + mxu(value, spread)
-    arrivals = devices * rows_dest
-    labels = jnp.concatenate([labels] * (arrivals // LANES), axis=1)
-    row_id = iota(labels.shape, 0)
-    lane_id = iota(labels.shape, 1)
-    labels = jnp.sum(
-        jnp.where(row_id == lane_id // (rows_dest * per_row), labels, 0.0), axis=0, keepdims=True
+    labels = jnp.concatenate([labels] * (plane_lanes // LANES), axis=1)
+    wanted = plane * (plane_size // per_row) + div(
+        iota((row_count, plane_lanes), 1), rows_dest * per_row
     )
-    out_id = iota((SEG_PER * part, arrivals), 0)
-    lane_id = iota((SEG_PER * part, arrivals), 1)
-    chosen = (labels == (out_id // part + 1).astype(jnp.float32)) & (
-        out_id % part == lane_id % part
-    )
-    summing = jnp.where(chosen, 1.0, 0.0)
-    counts = jnp.sum(summing, axis=1, keepdims=True)
-    out_scale = 1.0 / jnp.sqrt(jnp.maximum(counts, 1.0))
-    summing = summing.astype(jnp.bfloat16)
-
-    tile_owners = owner_rows[pl.ds(me // per_row, 1), :]
+    wanted = iota((row_count, plane_lanes), 0) == wanted
+    out_id = iota((out_rows, plane_lanes), 0)
+    lane_id = iota((out_rows, plane_lanes), 1)
+    aligned = mod(out_id, part) == mod(lane_id, part)
+    slot_id = (div(out_id, part) + 1).astype(jnp.float32)
+    for step in range(steps):
+        rows = labels[step * row_count : (step + 1) * row_count]
+        label = jnp.sum(jnp.where(wanted, rows, 0.0), axis=0, keepdims=True)
+        summing[step] = onehot((label == slot_id) & aligned)
+
+    tile_owners = owner_rows[pl.ds(div(me, per_row), 1), :]
     bucket_id = iota((bucket_rows, LANES), 0)
-    held = bucket_id // CAP == tile_owners
+    held = div(bucket_id, CAP) == tile_owners
     tile_ranks = mxu(onehot(held), earlier)
-    placed = onehot(held & (tile_ranks == (bucket_id % CAP).astype(jnp.float32)))
+    placed = onehot(held & (tile_ranks == mod(bucket_id, CAP).astype(jnp.float32)))
     fold = onehot(
-        (lane_a // tile == lax.rem(me, per_row)) & (lane_a % tile == lane_b % tile)
+        (div(lane_a, tile) == lax.rem(me, per_row)) & (mod(lane_a, tile) == mod(lane_b, tile))
     )
     placed = mxu(placed, fold)
-    placed = jnp.concatenate([placed] * blocks, axis=0)
-    placed = jnp.where(
-        iota(placed.shape, 0) // bucket_rows == iota(placed.shape, 1) // tile, placed, 0.0
+    lane_block = div(iota((bucket_rows, LANES), 1), tile)
+    placed = jnp.concatenate(
+        [jnp.where(lane_block == block, placed, 0.0) for block in range(blocks)], axis=0
     ).astype(jnp.bfloat16)
 
     own[...] = mxu(placed, white[...])
@@ -268,21 +309,44 @@
     sources[...] = total
 
     scale = 1.0 / math.sqrt(blocks * HALF)
-    steps = rcv_count // OWNERS_STEP
     group_rows = src_count * rows_dest
 
-    def bucket_copy(owner, place):
+    def bucket_copy(chunk, other):
         return pltpu.make_async_remote_copy(
-            src_ref=buckets.at[owner * src_count + place],
-            dst_ref=arrived.at[me],
+            src_ref=buckets.at[chunk * plane_size + other],
+            dst_ref=arrived.at[chunk, spot],
             send_sem=bucket_send,
-            recv_sem=bucket_recv,
-            device_id=(owner, place),
+            recv_sem=bucket_recv.at[chunk],
+            device_id=(plane * OWNERS_STEP + other // src_count, lax.rem(other, src_count)),
             device_id_type=MESH,
         )
 
+    def sum_copy(chunk):
+        return pltpu.make_async_remote_copy(
+            src_ref=partial.at[chunk],
+            dst_ref=arrived_sums.at[plane],
+            send_sem=sum_send,
+            recv_sem=sum_recv,
+            device_id=(chunk * OWNERS_STEP + owner_here, pos),
+            device_id_type=MESH,
+        )
+
+    def chunk_of(step):
+        return lax.rem(plane + 1 + step, steps)
+
+    def plane_sum(chunk):
+        arrived[chunk, pl.ds(spot, 1)] = buckets[pl.ds(chunk * plane_size + spot, 1)]
+        landed = arrived.at[chunk, pl.ds(0, plane_size - 1)]
+        pltpu.make_async_copy(landed, landed, bucket_recv.at[chunk]).wait()
+        return mxu(summing[chunk], arrived[chunk].reshape(plane_lanes, LAGS))
+
+    def pass_on(step):
+        chunk = chunk_of(step)
+        partial[chunk] = plane_sum(chunk).astype(jnp.bfloat16)
+        sum_copy(chunk).start()
+
     def owner_step(step, carry):
-        chunk = lax.rem(rcv // OWNERS_STEP + 1 + step, steps)
+        chunk = chunk_of(step)
 
         def cross_step(index, inner):
             re_cols = pl.ds(pl.multiple_of(index * LANES, LANES), LANES)
@@ -320,30 +384,37 @@
 
         lax.fori_loop(0, HALF // LANES, cross_step, 0)
         rows = (mxu(cross[...], lags[...]) * scale).astype(jnp.bfloat16)
-        dests = OWNERS_STEP * src_count
-        buckets[pl.ds(chunk * dests, dests)] = rows.reshape(dests, rows_dest, LAGS)
+        buckets[pl.ds(chunk * plane_size, plane_size)] = rows.reshape(plane_size, rows_dest, LAGS)
 
         def send(index, inner):
-            dest = chunk * dests + index
-
-            @pl.when(dest != me)
-            def _():
-                bucket_copy(dest // src_count, lax.rem(dest, src_count)).start()
-
+            bucket_copy(chunk, lax.rem(spot + index, plane_size)).start()
             return inner
 
-        lax.fori_loop(0, dests, send, 0)
+        lax.fori_loop(1, plane_size, send, 0)
+
+        @pl.when(step >= DELAY)
+        def _():
+            pass_on(step - DELAY)
+
         return carry
 
     lax.fori_loop(0, steps, owner_step, 0)
-    arrived[pl.ds(me, 1)] = buckets[pl.ds(me, 1)]
-
-    others = pl.ds(0, devices - 1)
-    pltpu.make_async_copy(arrived.at[others], arrived.at[others], bucket_recv).wait()
-    stacked = mxu(summing, arrived[...].reshape(arrivals, LAGS)) * out_scale
-    out[...] = stacked.reshape(SEG_PER, part, LAGS)
-
-    pltpu.make_async_copy(buckets.at[others], buckets.at[others], bucket_send).wait()
+    for step in range(steps - DELAY, steps - 1):
+        pass_on(step)
+    stacked = plane_sum(plane)
+
+    others = pl.ds(0, steps - 1)
+    landed = arrived_sums.at[others]
+    pltpu.make_async_copy(landed, landed, sum_recv).wait()
+    arrived_sums[plane] = jnp.zeros((out_rows, LAGS), jnp.bfloat16)
+    for step in range(steps):
+        stacked = stacked + arrived_sums[step].astype(jnp.float32)
+    out[...] = (stacked * out_scale).reshape(SEG_PER, part, LAGS)
+
+    sent = partial.at[others]
+    pltpu.make_async_copy(sent, sent, sum_send).wait()
+    sent = buckets.at[pl.ds(0, steps * (plane_size - 1))]
+    pltpu.make_async_copy(sent, sent, bucket_send).wait()
     for step in range(1, src_count):
         start_copy(step).wait_send()
         source_copy(step).wait_send()
@@ -357,6 +428,8 @@
     part = window // src_count
     rows_dest = CAP * part
     bucket_rows = rcv_count * CAP
+    steps = rcv_count // OWNERS_STEP
+    plane_size = OWNERS_STEP * src_count
     segments = channel_segment.reshape(-1, LANES)
     tables = jnp.asarray(dft_tables())
     lag_rows = jnp.asarray(lag_table())
@@ -377,6 +450,7 @@
             pltpu.VMEM(tables.shape, bf16),
             pltpu.VMEM(lag_rows.shape, bf16),
             pltpu.VMEM(segments.shape, i32),
+            pltpu.VMEM((steps, SEG_PER * part, plane_size * rows_dest), bf16),
             pltpu.VMEM((8, LANES), i32),
             pltpu.VMEM((src_count - 1, 8, LANES), i32),
             pltpu.VMEM((blocks * tile, NFFT), bf16),
@@ -386,12 +460,16 @@
             pltpu.VMEM((blocks * window, NFFT), f32),
             pltpu.VMEM((OWNERS_STEP * src_count * rows_dest, NFFT), bf16),
             pltpu.VMEM((devices, rows_dest, LAGS), bf16),
-            pltpu.VMEM((devices, rows_dest, LAGS), bf16),
+            pltpu.VMEM((steps, plane_size, rows_dest, LAGS), bf16),
+            pltpu.VMEM((steps, SEG_PER * part, LAGS), bf16),
+            pltpu.VMEM((steps, SEG_PER * part, LAGS), bf16),
             dma((5,)),
             dma((src_count - 1,)),
             dma((src_count - 1,)),
             dma((src_count - 1,)),
             dma((src_count - 1,)),
+            dma,
+            dma((steps,)),
             dma,
             dma,
         ],

time: 22.3 us -> 24 us (1.076)
  Pallas kernels: 20 us -> 21.7 us
    pallas_call x1, Pallas kernels: 20 us -> 21.7 us  [on_device(): pl.pallas_call(functools.partial(kernel, rcv_count, src_count, tile, bloc...]
where the time goes in v3:
time: 24 us; the launch traced here: 23.7 us
  Pallas kernels  21.7 us (90%)
  local copies, waits for them, and re-layouts  1.38 us (6%)
  between operations  0.66 us (3%)
    pallas_call x1, Pallas kernels, on_device(): pl.pallas_call(functools.partial(kernel, rcv_count, src_count, tile, bloc...  21.7 us
    unnamed x1, local copies, waits for them, and re-layouts  1.38 us

profile of v3, /device:TPU:0, one launch (start us, length us, event | category | flops | bytes accessed | tf_op | source)
XLA Modules:
  0.0 23.7 jit_solution(7446747138632000342)
XLA Ops:
  0.7 21.7 %shard_map.64 = f32[4,8,256]{2,1,0:T(8,128)} custom-call(s32[1]{0:T(128)S(6)} %copy.8.window_start, s32[64]{0:T(128)} %segment_row_in.1, s32[8,128]{1,0:T(8,128)} %bitcast.1, f32[32,4096]{1,0:T(8,128)} %records.1, bf16[2,1536,256]{2,1,0:T(8,128)(2,1)} %constant.4.clone.tables, bf16[1024,256]{1,0:T(8,128)(2,1)} %constant.5.clone.lag_rows), custom_call_target="tpu_custom_call" | custom-call | tf_op jit(solution)/shard_map/pallas_call | solution.py:441
  22.4 1.4 %copy.9 = f32[4,8,256]{2,1,0:T(8,128)} copy(f32[4,8,256]{2,1,0:T(8,128)} %shard_map.64) | data formatting | bytes 65536

commit v4 on v2

--- a/solution.py
+++ b/solution.py
@@ -18,6 +18,7 @@
 SEG_PER = 4
 LANES = 128
 OWNERS_STEP = 4
+OWNERS_SEND = 8
 MESH = pl.DeviceIdType.MESH
 ORDER = np.concatenate([np.arange(r, HALF, 4) for r in (0, 2, 1, 3)])
 
@@ -44,6 +45,14 @@
 
 def iota(shape, axis):
     return lax.broadcasted_iota(jnp.int32, shape, axis)
+
+
+def div(a, b):
+    return lax.shift_right_logical(a, b.bit_length() - 1) if b & (b - 1) == 0 else a // b
+
+
+def mod(a, b):
+    return a & (b - 1) if b & (b - 1) == 0 else a % b
 
 
 def onehot(mask):
@@ -72,6 +81,8 @@
     table,
     lags,
     owner_rows,
+    summing,
+    out_scale,
     starts_out,
     starts_in,
     white,
@@ -113,11 +124,11 @@
     barrier = pltpu.get_barrier_semaphore()
 
     def greet(step, carry):
-        other = lax.rem(me + step, devices)
+        other = mod(me + step, devices)
         pl.semaphore_signal(
             barrier,
             inc=1,
-            device_id=(other // src_count, lax.rem(other, src_count)),
+            device_id=(div(other, src_count), mod(other, src_count)),
             device_id_type=MESH,
         )
         return carry
@@ -177,29 +188,35 @@
     factor = lax.rsqrt(powers + 0.1 * mean_power + 1e-06)
     white[...] = jnp.concatenate([real * factor, imag * factor], axis=1).astype(jnp.bfloat16)
 
-    def source_copy(step):
+    def source_copy(step, column):
         other = lax.rem(pos + step, src_count)
         return pltpu.make_async_remote_copy(
-            src_ref=sources_out.at[step - 1],
-            dst_ref=sources_in.at[step - 1],
-            send_sem=source_send.at[step - 1],
-            recv_sem=source_recv.at[step - 1],
+            src_ref=sources_out.at[step - 1, column],
+            dst_ref=sources_in.at[step - 1, column],
+            send_sem=source_send.at[step - 1, column],
+            recv_sem=source_recv.at[step - 1, column],
             device_id=(rcv, other),
             device_id_type=MESH,
         )
 
+    columns = HALF // LANES
+    row_id = iota((blocks * window, LANES), 0)
+    lane_id = iota((blocks * window, LANES), 1)
+    same_block = div(row_id, window) == div(lane_id, tile)
+    offset = mod(row_id, window) - mod(lane_id, tile)
     for step in range(1, src_count):
         other = lax.rem(pos + step, src_count)
         start_copy(src_count - step).wait_recv()
         first_position = starts_in[src_count - step - 1, 0:1, :]
         my_place = pos - jnp.where(pos < other, 0, 1)
-        row_id = iota((blocks * window, LANES), 0)
-        lane_id = iota((blocks * window, LANES), 1)
-        asked = (first_position + row_id % window == my_place * tile + lane_id % tile) & (
-            row_id // window == lane_id // tile
-        )
-        sources_out[step - 1] = mxu(onehot(asked), white[...]).astype(jnp.bfloat16)
-        source_copy(step).start()
+        asked = onehot(same_block & (offset == my_place * tile - first_position))
+        for column in range(columns):
+            for half in range(2):
+                lanes = slice(half * HALF + column * LANES, half * HALF + (column + 1) * LANES)
+                sources_out[step - 1, column, :, half * LANES : (half + 1) * LANES] = mxu(
+                    asked, white[:, lanes]
+                ).astype(jnp.bfloat16)
+            source_copy(step, column).start()
 
     loads[2].wait()
     loads[3].wait()
@@ -211,11 +228,25 @@
     stack_rows = lax.fori_loop(
         0, segment_row.shape[0], look_up, jnp.zeros(all_segments.shape, jnp.int32), unroll=8
     )
-    owners = stack_rows // SEG_PER
-    slots = stack_rows - owners * SEG_PER
+    owners = div(stack_rows, SEG_PER)
+    slots = mod(stack_rows, SEG_PER)
     owner_rows[...] = owners
     lane_a, lane_b = iota((LANES, LANES), 0), iota((LANES, LANES), 1)
-    earlier = onehot((lane_a // tile == lane_b // tile) & (lane_a < lane_b))
+    earlier = onehot((div(lane_a, tile) == div(lane_b, tile)) & (lane_a < lane_b))
+
+    tile_owners = owner_rows[pl.ds(div(me, per_row), 1), :]
+    bucket_id = iota((bucket_rows, LANES), 0)
+    held = div(bucket_id, CAP) == tile_owners
+    tile_ranks = mxu(onehot(held), earlier)
+    placed = onehot(held & (tile_ranks == mod(bucket_id, CAP).astype(jnp.float32)))
+    fold = onehot(
+        (div(lane_a, tile) == lax.rem(me, per_row)) & (mod(lane_a, tile) == mod(lane_b, tile))
+    )
+    placed = mxu(placed, fold)
+    lane_block = div(iota((bucket_rows, LANES), 1), tile)
+    placed = jnp.concatenate(
+        [jnp.where(lane_block == block, placed, 0.0) for block in range(blocks)], axis=0
+    ).astype(jnp.bfloat16)
 
     mine = owners == rcv
     ranks = mxu(onehot(mine), earlier)
@@ -223,71 +254,42 @@
     for rank in range(CAP):
         value = jnp.where(mine & (ranks == rank), slots + 1, 0).astype(jnp.bfloat16)
         spread = onehot(
-            (lane_a // tile == lane_b // rows_dest % per_row) & (lane_b // part % CAP == rank)
+            (div(lane_a, tile) == mod(div(lane_b, rows_dest), per_row))
+            & (mod(div(lane_b, part), CAP) == rank)
         )
         labels = labels + mxu(value, spread)
     arrivals = devices * rows_dest
     labels = jnp.concatenate([labels] * (arrivals // LANES), axis=1)
-    row_id = iota(labels.shape, 0)
-    lane_id = iota(labels.shape, 1)
-    labels = jnp.sum(
-        jnp.where(row_id == lane_id // (rows_dest * per_row), labels, 0.0), axis=0, keepdims=True
+    wanted = iota(labels.shape, 0) == div(iota(labels.shape, 1), rows_dest * per_row)
+    labels = jnp.sum(jnp.where(wanted, labels, 0.0), axis=0, keepdims=True)
+    out_rows = SEG_PER * part
+    out_id = iota((out_rows, arrivals), 0)
+    lane_id = iota((out_rows, arrivals), 1)
+    chosen = (labels == (div(out_id, part) + 1).astype(jnp.float32)) & (
+        mod(out_id, part) == mod(lane_id, part)
     )
-    out_id = iota((SEG_PER * part, arrivals), 0)
-    lane_id = iota((SEG_PER * part, arrivals), 1)
-    chosen = (labels == (out_id // part + 1).astype(jnp.float32)) & (
-        out_id % part == lane_id % part
+    chosen = jnp.where(chosen, 1.0, 0.0)
+    counts = jnp.sum(chosen, axis=1, keepdims=True)
+    out_scale[...] = jnp.broadcast_to(
+        1.0 / jnp.sqrt(jnp.maximum(counts, 1.0)), (out_rows, LAGS)
     )
-    summing = jnp.where(chosen, 1.0, 0.0)
-    counts = jnp.sum(summing, axis=1, keepdims=True)
-    out_scale = 1.0 / jnp.sqrt(jnp.maximum(counts, 1.0))
-    summing = summing.astype(jnp.bfloat16)
-
-    tile_owners = owner_rows[pl.ds(me // per_row, 1), :]
-    bucket_id = iota((bucket_rows, LANES), 0)
-    held = bucket_id // CAP == tile_owners
-    tile_ranks = mxu(onehot(held), earlier)
-    placed = onehot(held & (tile_ranks == (bucket_id % CAP).astype(jnp.float32)))
-    fold = onehot(
-        (lane_a // tile == lax.rem(me, per_row)) & (lane_a % tile == lane_b % tile)
-    )
-    placed = mxu(placed, fold)
-    placed = jnp.concatenate([placed] * blocks, axis=0)
-    placed = jnp.where(
-        iota(placed.shape, 0) // bucket_rows == iota(placed.shape, 1) // tile, placed, 0.0
-    ).astype(jnp.bfloat16)
+    summing[...] = chosen.astype(jnp.bfloat16)
 
     own[...] = mxu(placed, white[...])
 
-    loads[4].wait()
-    for step in range(1, src_count):
-        source_copy(step).wait_recv()
-    total = sources_in[0].astype(jnp.float32)
-    for step in range(2, src_count):
-        total = total + sources_in[step - 1].astype(jnp.float32)
-    sources[...] = total
-
-    scale = 1.0 / math.sqrt(blocks * HALF)
-    steps = rcv_count // OWNERS_STEP
+    group = OWNERS_STEP * CAP
     group_rows = src_count * rows_dest
-
-    def bucket_copy(owner, place):
-        return pltpu.make_async_remote_copy(
-            src_ref=buckets.at[owner * src_count + place],
-            dst_ref=arrived.at[me],
-            send_sem=bucket_send,
-            recv_sem=bucket_recv,
-            device_id=(owner, place),
-            device_id_type=MESH,
-        )
-
-    def owner_step(step, carry):
-        chunk = lax.rem(rcv // OWNERS_STEP + 1 + step, steps)
-
-        def cross_step(index, inner):
-            re_cols = pl.ds(pl.multiple_of(index * LANES, LANES), LANES)
-            im_cols = pl.ds(pl.multiple_of(HALF + index * LANES, LANES), LANES)
-            group = OWNERS_STEP * CAP
+    for column in range(columns):
+        re_cols = slice(column * LANES, (column + 1) * LANES)
+        im_cols = slice(HALF + column * LANES, HALF + (column + 1) * LANES)
+        for step in range(1, src_count):
+            source_copy(step, column).wait_recv()
+        total = sources_in[0, column].astype(jnp.float32)
+        for step in range(2, src_count):
+            total = total + sources_in[step - 1, column].astype(jnp.float32)
+        sources[...] = total
+
+        def cross_step(chunk, carry):
             left = []
             for block in range(blocks):
                 first_row = pl.multiple_of(block * bucket_rows + chunk * group, group)
@@ -297,7 +299,7 @@
                 right = []
                 for block in range(blocks):
                     rows = slice(block * window + place * part, block * window + (place + 1) * part)
-                    right.append((sources[rows, re_cols], sources[rows, im_cols]))
+                    right.append((sources[rows, :LANES], sources[rows, LANES:]))
                 for owner in range(OWNERS_STEP):
                     reals, imags = [], []
                     for rank in range(CAP):
@@ -312,27 +314,45 @@
                             im_sum = im_term if im_sum is None else im_sum + im_term
                         reals.append(re_sum)
                         imags.append(im_sum)
-                    at = owner * group_rows + place * rows_dest
-                    rows = slice(at, at + rows_dest)
+                    at = (chunk * OWNERS_STEP + owner) * group_rows + place * rows_dest
+                    rows = pl.ds(pl.multiple_of(at, rows_dest), rows_dest)
                     cross[rows, re_cols] = jnp.concatenate(reals, axis=0).astype(jnp.bfloat16)
                     cross[rows, im_cols] = jnp.concatenate(imags, axis=0).astype(jnp.bfloat16)
-            return inner
-
-        lax.fori_loop(0, HALF // LANES, cross_step, 0)
-        rows = (mxu(cross[...], lags[...]) * scale).astype(jnp.bfloat16)
-        dests = OWNERS_STEP * src_count
-        buckets[pl.ds(chunk * dests, dests)] = rows.reshape(dests, rows_dest, LAGS)
+            return carry
+
+        lax.fori_loop(0, rcv_count // OWNERS_STEP, cross_step, 0)
+
+    loads[4].wait()
+    scale = 1.0 / math.sqrt(blocks * HALF)
+    dests = OWNERS_SEND * src_count
+    steps = devices // dests
+
+    def bucket_copy(dest):
+        return pltpu.make_async_remote_copy(
+            src_ref=buckets.at[dest],
+            dst_ref=arrived.at[me],
+            send_sem=bucket_send,
+            recv_sem=bucket_recv,
+            device_id=(div(dest, src_count), mod(dest, src_count)),
+            device_id_type=MESH,
+        )
+
+    def owner_step(step, carry):
+        first_dest = lax.rem(div(me, dests) + 1 + step, steps) * dests
+        rows = pl.ds(pl.multiple_of(first_dest * rows_dest, rows_dest), dests * rows_dest)
+        result = (mxu(cross[rows, :], lags[...]) * scale).astype(jnp.bfloat16)
+        buckets[pl.ds(first_dest, dests)] = result.reshape(dests, rows_dest, LAGS)
 
         def send(index, inner):
-            dest = chunk * dests + index
+            dest = first_dest + mod(me + index, dests)
 
             @pl.when(dest != me)
             def _():
-                bucket_copy(dest // src_count, lax.rem(dest, src_count)).start()
+                bucket_copy(dest).start()
 
             return inner
 
-        lax.fori_loop(0, dests, send, 0)
+        lax.fori_loop(1, dests + 1, send, 0)
         return carry
 
     lax.fori_loop(0, steps, owner_step, 0)
@@ -340,13 +360,14 @@
 
     others = pl.ds(0, devices - 1)
     pltpu.make_async_copy(arrived.at[others], arrived.at[others], bucket_recv).wait()
-    stacked = mxu(summing, arrived[...].reshape(arrivals, LAGS)) * out_scale
+    stacked = mxu(summing[...], arrived[...].reshape(arrivals, LAGS)) * out_scale[...]
     out[...] = stacked.reshape(SEG_PER, part, LAGS)
 
     pltpu.make_async_copy(buckets.at[others], buckets.at[others], bucket_send).wait()
     for step in range(1, src_count):
         start_copy(step).wait_send()
-        source_copy(step).wait_send()
+        for column in range(columns):
+            source_copy(step, column).wait_send()
 
 
 def on_device(rcv_count, src_count, records, window_start, channel_segment, segment_row):
@@ -357,6 +378,7 @@
     part = window // src_count
     rows_dest = CAP * part
     bucket_rows = rcv_count * CAP
+    columns = HALF // LANES
     segments = channel_segment.reshape(-1, LANES)
     tables = jnp.asarray(dft_tables())
     lag_rows = jnp.asarray(lag_table())
@@ -377,21 +399,23 @@
             pltpu.VMEM(tables.shape, bf16),
             pltpu.VMEM(lag_rows.shape, bf16),
             pltpu.VMEM(segments.shape, i32),
+            pltpu.VMEM((SEG_PER * part, devices * rows_dest), bf16),
+            pltpu.VMEM((SEG_PER * part, LAGS), f32),
             pltpu.VMEM((8, LANES), i32),
             pltpu.VMEM((src_count - 1, 8, LANES), i32),
             pltpu.VMEM((blocks * tile, NFFT), bf16),
-            pltpu.VMEM((src_count - 1, blocks * window, NFFT), bf16),
-            pltpu.VMEM((src_count - 1, blocks * window, NFFT), bf16),
+            pltpu.VMEM((src_count - 1, columns, blocks * window, 2 * LANES), bf16),
+            pltpu.VMEM((src_count - 1, columns, blocks * window, 2 * LANES), bf16),
             pltpu.VMEM((blocks * bucket_rows, NFFT), f32),
-            pltpu.VMEM((blocks * window, NFFT), f32),
-            pltpu.VMEM((OWNERS_STEP * src_count * rows_dest, NFFT), bf16),
+            pltpu.VMEM((blocks * window, 2 * LANES), f32),
+            pltpu.VMEM((devices * rows_dest, NFFT), bf16),
             pltpu.VMEM((devices, rows_dest, LAGS), bf16),
             pltpu.VMEM((devices, rows_dest, LAGS), bf16),
             dma((5,)),
             dma((src_count - 1,)),
             dma((src_count - 1,)),
-            dma((src_count - 1,)),
-            dma((src_count - 1,)),
+            dma((src_count - 1, columns)),
+            dma((src_count - 1, columns)),
             dma,
             dma,
         ],

time: 22.3 us -> 23.2 us (1.040)
  Pallas kernels: 20 us -> 21 us
    pallas_call x1, Pallas kernels: 20 us -> 21 us  [on_device(): pl.pallas_call(functools.partial(kernel, rcv_count, src_count, tile, bloc...]
where the time goes in v4:
time: 23.2 us; the launch traced here: 23 us
  Pallas kernels  21 us (91%)
  local copies, waits for them, and re-layouts  1.38 us (6%)
  between operations  0.66 us (3%)
    pallas_call x1, Pallas kernels, on_device(): pl.pallas_call(functools.partial(kernel, rcv_count, src_count, tile, bloc...  21 us
    unnamed x1, local copies, waits for them, and re-layouts  1.38 us

profile of v4, /device:TPU:0, one launch (start us, length us, event | category | flops | bytes accessed | tf_op | source)
XLA Modules:
  0.0 23.0 jit_solution(13991328469409948759)
XLA Ops:
  0.7 21.0 %shard_map.64 = f32[4,8,256]{2,1,0:T(8,128)} custom-call(s32[1]{0:T(128)S(6)} %copy.8.window_start, s32[64]{0:T(128)} %segment_row_in.1, s32[8,128]{1,0:T(8,128)} %bitcast.1, f32[32,4096]{1,0:T(8,128)} %records.1, bf16[2,1536,256]{2,1,0:T(8,128)(2,1)} %constant.4.clone.tables, bf16[1024,256]{1,0:T(8,128)(2,1)} %constant.5.clone.lag_rows), custom_call_target="tpu_custom_call" | custom-call | tf_op jit(solution)/shard_map/pallas_call | solution.py:390
  21.6 1.4 %copy.9 = f32[4,8,256]{2,1,0:T(8,128)} copy(f32[4,8,256]{2,1,0:T(8,128)} %shard_map.64) | data formatting | bytes 65536

commit v5 on v2

--- a/solution.py
+++ b/solution.py
@@ -396,9 +396,15 @@
             dma,
         ],
         compiler_params=pltpu.CompilerParams(
-            collective_id=0, has_side_effects=True, vmem_limit_bytes=62 * 1024 * 1024
+            collective_id=0, has_side_effects=True, vmem_limit_bytes=48 * 1024 * 1024
         ),
-    )(window_start, segment_row, segments, records, tables, lag_rows)
+    )(
+        window_start,
+        *(
+            pltpu.with_memory_space_constraint(operand, pltpu.HBM)
+            for operand in (segment_row, segments, records, tables, lag_rows)
+        ),
+    )
 
 
 def solution(mesh):

time: 22.3 us -> 20.9 us (0.937)
  local copies, waits for them, and re-layouts: 1.38 us -> 0.62 us
  Pallas kernels: 20 us -> 19.4 us
    unnamed x1, local copies, waits for them, and re-layouts: 1.38 us -> 0.62 us
    pallas_call x1, Pallas kernels: 20 us -> 19.4 us  [on_device(): pl.pallas_call(functools.partial(kernel, rcv_count, src_count, tile, bloc...]
where the time goes in v5:
time: 20.9 us; the launch traced here: 20.7 us
  Pallas kernels  19.4 us (93%)
  between operations  0.66 us (3%)
  local copies, waits for them, and re-layouts  0.62 us (3%)
    pallas_call x1, Pallas kernels, on_device(): pl.pallas_call(functools.partial(kernel, rcv_count, src_count, tile, bloc...  19.4 us
    unnamed x1, local copies, waits for them, and re-layouts  0.62 us

profile of v5, /device:TPU:0, one launch (start us, length us, event | category | flops | bytes accessed | tf_op | source)
XLA Modules:
  0.0 20.7 jit_solution(6365219124912562680)
XLA Ops:
  0.7 19.4 %shard_map.64 = f32[4,8,256]{2,1,0:T(8,128)S(1)} custom-call(s32[1]{0:T(128)S(6)} %copy.8.window_start, s32[64]{0:T(128)} %segment_row_in.1, s32[8,128]{1,0:T(8,128)} %bitcast.1, f32[32,4096]{1,0:T(8,128)} %records.1, bf16[2,1536,256]{2,1,0:T(8,128)(2,1)} %constant.4.clone.tables, bf16[1024,256]{1,0:T(8,128)(2,1)} %constant.5.clone.lag_rows), custom_call_target="tpu_custom_call" | custom-call | tf_op jit(solution)/shard_map/pallas_call | solution.py:368
  20.1 0.6 %copy.9 = f32[4,8,256]{2,1,0:T(8,128)} copy(f32[4,8,256]{2,1,0:T(8,128)S(1)} %shard_map.64) | data formatting | bytes 65536

commit v6 on v5

--- a/solution.py
+++ b/solution.py
@@ -44,6 +44,14 @@
 
 def iota(shape, axis):
     return lax.broadcasted_iota(jnp.int32, shape, axis)
+
+
+def div(a, b):
+    return lax.shift_right_logical(a, b.bit_length() - 1) if b & (b - 1) == 0 else a // b
+
+
+def mod(a, b):
+    return a & (b - 1) if b & (b - 1) == 0 else a % b
 
 
 def onehot(mask):
@@ -188,16 +196,16 @@
             device_id_type=MESH,
         )
 
+    row_id = iota((blocks * window, LANES), 0)
+    lane_id = iota((blocks * window, LANES), 1)
+    same_block = div(row_id, window) == div(lane_id, tile)
+    offset = mod(row_id, window) - mod(lane_id, tile)
     for step in range(1, src_count):
         other = lax.rem(pos + step, src_count)
         start_copy(src_count - step).wait_recv()
         first_position = starts_in[src_count - step - 1, 0:1, :]
         my_place = pos - jnp.where(pos < other, 0, 1)
-        row_id = iota((blocks * window, LANES), 0)
-        lane_id = iota((blocks * window, LANES), 1)
-        asked = (first_position + row_id % window == my_place * tile + lane_id % tile) & (
-            row_id // window == lane_id // tile
-        )
+        asked = same_block & (offset == my_place * tile - first_position)
         sources_out[step - 1] = mxu(onehot(asked), white[...]).astype(jnp.bfloat16)
         source_copy(step).start()
 
@@ -211,11 +219,11 @@
     stack_rows = lax.fori_loop(
         0, segment_row.shape[0], look_up, jnp.zeros(all_segments.shape, jnp.int32), unroll=8
     )
-    owners = stack_rows // SEG_PER
-    slots = stack_rows - owners * SEG_PER
+    owners = div(stack_rows, SEG_PER)
+    slots = mod(stack_rows, SEG_PER)
     owner_rows[...] = owners
     lane_a, lane_b = iota((LANES, LANES), 0), iota((LANES, LANES), 1)
-    earlier = onehot((lane_a // tile == lane_b // tile) & (lane_a < lane_b))
+    earlier = onehot((div(lane_a, tile) == div(lane_b, tile)) & (lane_a < lane_b))
 
     mine = owners == rcv
     ranks = mxu(onehot(mine), earlier)
@@ -223,7 +231,8 @@
     for rank in range(CAP):
         value = jnp.where(mine & (ranks == rank), slots + 1, 0).astype(jnp.bfloat16)
         spread = onehot(
-            (lane_a // tile == lane_b // rows_dest % per_row) & (lane_b // part % CAP == rank)
+            (div(lane_a, tile) == mod(div(lane_b, rows_dest), per_row))
+            & (mod(div(lane_b, part), CAP) == rank)
         )
         labels = labels + mxu(value, spread)
     arrivals = devices * rows_dest
@@ -231,12 +240,12 @@
     row_id = iota(labels.shape, 0)
     lane_id = iota(labels.shape, 1)
     labels = jnp.sum(
-        jnp.where(row_id == lane_id // (rows_dest * per_row), labels, 0.0), axis=0, keepdims=True
+        jnp.where(row_id == div(lane_id, rows_dest * per_row), labels, 0.0), axis=0, keepdims=True
     )
     out_id = iota((SEG_PER * part, arrivals), 0)
     lane_id = iota((SEG_PER * part, arrivals), 1)
-    chosen = (labels == (out_id // part + 1).astype(jnp.float32)) & (
-        out_id % part == lane_id % part
+    chosen = (labels == (div(out_id, part) + 1).astype(jnp.float32)) & (
+        mod(out_id, part) == mod(lane_id, part)
     )
     summing = jnp.where(chosen, 1.0, 0.0)
     counts = jnp.sum(summing, axis=1, keepdims=True)
@@ -245,16 +254,16 @@
 
     tile_owners = owner_rows[pl.ds(me // per_row, 1), :]
     bucket_id = iota((bucket_rows, LANES), 0)
-    held = bucket_id // CAP == tile_owners
+    held = div(bucket_id, CAP) == tile_owners
     tile_ranks = mxu(onehot(held), earlier)
-    placed = onehot(held & (tile_ranks == (bucket_id % CAP).astype(jnp.float32)))
+    placed = onehot(held & (tile_ranks == mod(bucket_id, CAP).astype(jnp.float32)))
     fold = onehot(
-        (lane_a // tile == lax.rem(me, per_row)) & (lane_a % tile == lane_b % tile)
+        (div(lane_a, tile) == lax.rem(me, per_row)) & (mod(lane_a, tile) == mod(lane_b, tile))
     )
     placed = mxu(placed, fold)
     placed = jnp.concatenate([placed] * blocks, axis=0)
     placed = jnp.where(
-        iota(placed.shape, 0) // bucket_rows == iota(placed.shape, 1) // tile, placed, 0.0
+        div(iota(placed.shape, 0), bucket_rows) == div(iota(placed.shape, 1), tile), placed, 0.0
     ).astype(jnp.bfloat16)
 
     own[...] = mxu(placed, white[...])

time: 20.9 us -> 20.9 us (level)
  no operation moved by 1% of the time
where the time goes in v6:
time: 20.9 us; the launch traced here: 20.7 us
  Pallas kernels  19.4 us (93%)
  between operations  0.66 us (3%)
  local copies, waits for them, and re-layouts  0.62 us (3%)
    pallas_call x1, Pallas kernels, on_device(): pl.pallas_call(functools.partial(kernel, rcv_count, src_count, tile, bloc...  19.4 us
    unnamed x1, local copies, waits for them, and re-layouts  0.62 us

profile of v6, /device:TPU:0, one launch (start us, length us, event | category | flops | bytes accessed | tf_op | source)
XLA Modules:
  0.0 20.7 jit_solution(16042131166858013984)
XLA Ops:
  0.7 19.4 %shard_map.64 = f32[4,8,256]{2,1,0:T(8,128)S(1)} custom-call(s32[1]{0:T(128)S(6)} %copy.8.window_start, s32[64]{0:T(128)} %segment_row_in.1, s32[8,128]{1,0:T(8,128)} %bitcast.1, f32[32,4096]{1,0:T(8,128)} %records.1, bf16[2,1536,256]{2,1,0:T(8,128)(2,1)} %constant.4.clone.tables, bf16[1024,256]{1,0:T(8,128)(2,1)} %constant.5.clone.lag_rows), custom_call_target="tpu_custom_call" | custom-call | tf_op jit(solution)/shard_map/pallas_call | solution.py:377
  20.1 0.6 %copy.9 = f32[4,8,256]{2,1,0:T(8,128)} copy(f32[4,8,256]{2,1,0:T(8,128)S(1)} %shard_map.64) | data formatting | bytes 65536
